TPU v7x, 512 devices: a whole 4x8x8 slice. The times are simulated.
512 devices in a mesh: box: 128 (over z, y, core), sub: 4 (over x).
Axes of the slice: x: 4, y: 8, z: 8, core: 2. Of those that a mesh axis runs over, the one named last changes fastest.
Arguments:
- rhs_points: bfloat16 [131072, 512], P(('box', 'sub')), may hold values from -6 to 6
- interp: bfloat16 [131072, 256], P(('box', 'sub')), may hold values from -0.375 to 0.375
- skel_count: int32 [128], P('box'), may hold values from 128 to 256, as said below
- butterfly: float32 [3, 32768, 512], P(None, 'box'), may hold values from -0.25 to 0.25
- project: float32 [32768, 256], P('box'), may hold values from -0.375 to 0.375
- root_inverse: float32 [256, 256], replicated, may hold values from -0.03125 to 0.03125
Outputs:
- x_points: float32 [131072, 512], P(('box', 'sub'))
Inputs may be any that keep to these rules, and one draw needn't show every extreme that they name: `skel_count`: each box has between 128 and 256 live skeleton rows; some box has exactly 256.
All inputs are finite; a program needn't handle non-finite values.
Results may differ from a plain program's by a relative error of at most 0.0028.
Values may be sent and summed in bfloat16 or wider, within the bound.
A program may use at most 64 MiB of HBM per device.

v0:
```python
import jax
import jax.numpy as jnp
from jax import lax
from jax.sharding import PartitionSpec as P


def swapped(value, axis, stride):
    return lax.ppermute(value, axis, [(i, i ^ 1 << stride) for i in range(lax.axis_size(axis))])


def times_left(matrix, block_rows):
    return jnp.dot(
        matrix, block_rows, precision=lax.Precision.HIGHEST, preferred_element_type=jnp.float32
    )


def transposed(matrix, block_rows):
    return lax.dot_general(
        matrix,
        block_rows,
        (((0,), (0,)), ((), ())),
        precision=lax.Precision.HIGHEST,
        preferred_element_type=jnp.float32,
    )


def local(rhs_points, interp, skel_count, butterfly, project, root_inverse):
    width = interp.shape[0]
    leaf_term = jnp.dot(interp, rhs_points, preferred_element_type=jnp.float32)
    skeleton = lax.psum(leaf_term, "sub")
    live_rows = (lax.broadcasted_iota(jnp.int32, (width, 1), 0) < skel_count[0]).astype(jnp.float32)
    upward = skeleton * live_rows
    top_bit = lax.axis_size("box").bit_length() - 1
    levels = butterfly.shape[0]
    for level in range(levels):
        bit_index = top_bit - levels + level
        own_block = butterfly[level, :, :width]
        cross_block = butterfly[level, :, width:]
        partner = swapped(upward, "box", bit_index)
        upward = times_left(own_block, upward) + times_left(cross_block, partner)
    root_sum = lax.psum(times_left(project, upward), "box")
    root_solution = times_left(root_inverse, root_sum)
    downward = upward - transposed(project, root_solution)
    for level in reversed(range(levels)):
        bit_index = top_bit - levels + level
        own_block = butterfly[level, :, :width]
        cross_block = butterfly[level, :, width:]
        sending = transposed(cross_block, downward)
        received = swapped(sending, "box", bit_index)
        downward = transposed(own_block, downward) + received
    back = (downward * live_rows).astype(jnp.bfloat16)
    update = lax.dot_general(
        interp, back, (((0,), (0,)), ((), ())), preferred_element_type=jnp.float32
    )
    return rhs_points.astype(jnp.float32) - update


def solution(mesh):
    in_specs = (
        P(("box", "sub"), None),
        P(("box", "sub"), None),
        P("box"),
        P(None, "box", None),
        P("box", None),
        P(),
    )
    out_specs = P(("box", "sub"), None)
    return jax.shard_map(local, mesh=mesh, in_specs=in_specs, out_specs=out_specs, check_vma=False)
```

profile of v0, /device:TPU:1, one launch (start us, length us, event | category | flops | bytes accessed | tf_op | source)
XLA Modules:
  0.0 420.7 jit_solution(4342632259621476199)
XLA Ops:
  6.5 0.0 copy-start
  6.5 0.0 copy-start.1
  6.5 0.0 all-reduce.3.cloned.1.call-start
  6.5 2.2 fusion.33
  8.7 0.0 all-reduce.3.cloned.1.call-update
  8.7 0.0 all-reduce.5.cloned.1.call-start
  9.4 57.3 %all-reduce.3.cloned.1.call-done = f32[256,512]{1,0:T(8,128)} async-done(((f32[256,512]{1,0:T(8,128)}), f32[256,512]{1,0:T(8,128)}) %all-reduce.3.cloned.1.call-update) | async-done | bytes 524304 | tf_op jit(solution)/shard_map/psum | solution.py:30
  66.8 1.1 broadcast_multiply_fusion
  67.9 3.4 collective-permute-start
  71.3 0.0 copy-done.1
  71.3 1.0 fusion.19
  72.4 8.1 %collective-permute-done = f32[256,512]{1,0:T(8,128)S(1)} collective-permute-done((f32[256,512]{1,0:T(8,128)S(1)}, f32[256,512]{1,0:T(8,128)S(1)}, u32[]{:S(2)}, u32[]{:S(2)}) %collective-permute-start) | collective-permute-done | bytes 524320 | tf_op jit(solution)/shard_map/ppermute | solution.py:8
  80.5 1.0 convolution_add_fusion.2
  81.5 4.5 %collective-permute-start.1 = (f32[256,512]{0,1:T(8,128)S(1)}, f32[256,512]{0,1:T(8,128)S(1)}, u32[]{:S(2)}, u32[]{:S(2)}) collective-permute-start(f32[256,512]{0,1:T(8,128)S(1)} %bitcast.84), channel_id=1, source_target_pairs={{0,128},{4,132},{8,136},{12,140},{16,144},{20,148},{24,152},{28,15... | collective-permute-start | bytes 1572872 | tf_op jit(solution)/shard_map/ppermute | solution.py:8
  86.1 0.6 fusion.14
  86.7 21.8 %collective-permute-done.1 = f32[256,512]{0,1:T(8,128)S(1)} collective-permute-done((f32[256,512]{0,1:T(8,128)S(1)}, f32[256,512]{0,1:T(8,128)S(1)}, u32[]{:S(2)}, u32[]{:S(2)}) %collective-permute-start.1) | collective-permute-done | bytes 524320 | tf_op jit(solution)/shard_map/ppermute | solution.py:8
  108.5 0.6 convolution_add_fusion.1
  109.1 8.6 %collective-permute-start.2 = (f32[256,512]{0,1:T(8,128)S(1)}, f32[256,512]{0,1:T(8,128)S(1)}, u32[]{:S(2)}, u32[]{:S(2)}) collective-permute-start(f32[256,512]{0,1:T(8,128)S(1)} %bitcast.85), channel_id=1, source_target_pairs={{0,256},{4,260},{8,264},{12,268},{16,272},{20,276},{24,280},{28,28... | collective-permute-start | bytes 1572872 | tf_op jit(solution)/shard_map/ppermute | solution.py:8
  117.8 0.6 fusion.9
  118.4 0.0 copy-start.4
  118.4 22.3 %collective-permute-done.2 = f32[256,512]{0,1:T(8,128)S(1)} collective-permute-done((f32[256,512]{0,1:T(8,128)S(1)}, f32[256,512]{0,1:T(8,128)S(1)}, u32[]{:S(2)}, u32[]{:S(2)}) %collective-permute-start.2) | collective-permute-done | bytes 524320 | tf_op jit(solution)/shard_map/ppermute | solution.py:8
  140.7 0.6 convolution_add_fusion
  141.4 0.0 copy-done
  141.4 1.4 convolution_bitcast_fusion.7
  142.8 0.0 all-reduce.5.cloned.1.call-update
  142.8 189.8 %all-reduce.5.cloned.1.call-done = f32[256,512]{0,1:T(8,128)} async-done(((f32[256,512]{0,1:T(8,128)}), f32[256,512]{0,1:T(8,128)}) %all-reduce.5.cloned.1.call-update) | async-done | bytes 524304 | tf_op jit(solution)/shard_map/psum | solution.py:41
  332.6 0.0 copy-done.4
  332.6 1.7 fusion.34
  334.3 0.6 convolution_subtract_fusion
  334.8 0.6 convolution_bitcast_fusion.5
  335.4 5.8 %collective-permute-start.3 = (f32[256,512]{0,1:T(8,128)S(1)}, f32[256,512]{0,1:T(8,128)S(1)}, u32[]{:S(2)}, u32[]{:S(2)}) collective-permute-start(f32[256,512]{0,1:T(8,128)S(1)} %convolution_bitcast_fusion.5), channel_id=1, source_target_pairs={{0,256},{4,260},{8,264},{12,268},{16,272},{20,276},{24,280},{28,28... | collective-permute-start | bytes 1572872 | tf_op jit(solution)/shard_map/ppermute | solution.py:8
  341.3 13.4 %collective-permute-done.3 = f32[256,512]{0,1:T(8,128)S(1)} collective-permute-done((f32[256,512]{0,1:T(8,128)S(1)}, f32[256,512]{0,1:T(8,128)S(1)}, u32[]{:S(2)}, u32[]{:S(2)}) %collective-permute-start.3) | collective-permute-done | bytes 524320 | tf_op jit(solution)/shard_map/ppermute | solution.py:8
  354.6 0.6 fusion.1
  355.2 0.6 convolution_bitcast_fusion.3
  355.8 0.0 copy-start.2
  355.8 15.9 %collective-permute-start.4 = (f32[256,512]{0,1:T(8,128)S(1)}, f32[256,512]{0,1:T(8,128)S(1)}, u32[]{:S(2)}, u32[]{:S(2)}) collective-permute-start(f32[256,512]{0,1:T(8,128)S(1)} %convolution_bitcast_fusion.3), channel_id=1, source_target_pairs={{0,128},{4,132},{8,136},{12,140},{16,144},{20,148},{24,152},{28,15... | collective-permute-start | bytes 1572872 | tf_op jit(solution)/shard_map/ppermute | solution.py:8
  371.7 23.3 %collective-permute-done.4 = f32[256,512]{0,1:T(8,128)S(1)} collective-permute-done((f32[256,512]{0,1:T(8,128)S(1)}, f32[256,512]{0,1:T(8,128)S(1)}, u32[]{:S(2)}, u32[]{:S(2)}) %collective-permute-start.4) | collective-permute-done | bytes 524320 | tf_op jit(solution)/shard_map/ppermute | solution.py:8
  395.0 0.6 fusion.2
  395.6 0.0 copy-start.3
  395.6 0.7 convolution_bitcast_fusion.1
  396.2 1.9 collective-permute-start.5
  398.2 0.0 copy-done.2
  398.2 0.1 copy.7
  398.3 12.5 %collective-permute-done.5 = f32[256,512]{1,0:T(8,128)} collective-permute-done((f32[256,512]{1,0:T(8,128)S(1)}, f32[256,512]{1,0:T(8,128)}, u32[]{:S(2)}, u32[]{:S(2)}) %collective-permute-start.5) | collective-permute-done | bytes 524320 | tf_op jit(solution)/shard_map/ppermute | solution.py:8
  410.9 1.7 fusion.5
  412.6 0.0 copy-done.3
  412.6 0.3 fusion
  412.8 1.0 copy.8
  (1 shorter events, 0.0 us)
Async XLA Ops:
  6.5 134.8 %copy-start = (f32[256,256]{1,0:T(8,128)S(1)}, f32[256,256]{1,0:T(8,128)}, u32[]{:S(2)}) copy-start(f32[256,256]{1,0:T(8,128)} %param.10) | copy-start | bytes 786436
  6.5 64.8 %copy-start.1 = (f32[3,256,512]{2,1,0:T(8,128)S(1)}, f32[3,256,512]{2,1,0:T(8,128)}, u32[]{:S(2)}) copy-start(f32[3,256,512]{2,1,0:T(8,128)} %param.9) | copy-start | bytes 4718596
  6.5 60.2 %all-reduce.3.cloned.1.call-start = ((), (), s32[]{:S(2)}) async-start(), calls=%async_computation | async-start | bytes 1048576 | tf_op jit(solution)/shard_map/psum | solution.py:30
  8.7 323.9 %all-reduce.5.cloned.1.call-start = ((), (), s32[]{:S(2)}) async-start(), calls=%async_computation.1 | async-start | bytes 1048576 | tf_op jit(solution)/shard_map/psum | solution.py:41
  67.9 12.6 %collective-permute-start = (f32[256,512]{1,0:T(8,128)S(1)}, f32[256,512]{1,0:T(8,128)S(1)}, u32[]{:S(2)}, u32[]{:S(2)}) collective-permute-start(f32[256,512]{1,0:T(8,128)S(1)} %broadcast_multiply_fusion), channel_id=1, source_target_pairs={{0,64},{4,68},{8,72},{12,76},{16,80},{20,84},{24,88},{28,92},{32,9... | collective-permute-start | bytes 1572872 | tf_op jit(solution)/shard_map/ppermute | solution.py:8
  81.5 27.0 %collective-permute-start.1 = (f32[256,512]{0,1:T(8,128)S(1)}, f32[256,512]{0,1:T(8,128)S(1)}, u32[]{:S(2)}, u32[]{:S(2)}) collective-permute-start(f32[256,512]{0,1:T(8,128)S(1)} %bitcast.84), channel_id=1, source_target_pairs={{0,128},{4,132},{8,136},{12,140},{16,144},{20,148},{24,152},{28,15... | collective-permute-start | bytes 1572872 | tf_op jit(solution)/shard_map/ppermute | solution.py:8
  109.1 31.6 %collective-permute-start.2 = (f32[256,512]{0,1:T(8,128)S(1)}, f32[256,512]{0,1:T(8,128)S(1)}, u32[]{:S(2)}, u32[]{:S(2)}) collective-permute-start(f32[256,512]{0,1:T(8,128)S(1)} %bitcast.85), channel_id=1, source_target_pairs={{0,256},{4,260},{8,264},{12,268},{16,272},{20,276},{24,280},{28,28... | collective-permute-start | bytes 1572872 | tf_op jit(solution)/shard_map/ppermute | solution.py:8
  118.4 214.2 %copy-start.4 = (f32[256,256]{1,0:T(8,128)S(1)}, f32[256,256]{1,0:T(8,128)}, u32[]{:S(2)}) copy-start(f32[256,256]{1,0:T(8,128)} %param.11) | copy-start | bytes 786436
  335.4 19.2 %collective-permute-start.3 = (f32[256,512]{0,1:T(8,128)S(1)}, f32[256,512]{0,1:T(8,128)S(1)}, u32[]{:S(2)}, u32[]{:S(2)}) collective-permute-start(f32[256,512]{0,1:T(8,128)S(1)} %convolution_bitcast_fusion.5), channel_id=1, source_target_pairs={{0,256},{4,260},{8,264},{12,268},{16,272},{20,276},{24,280},{28,28... | collective-permute-start | bytes 1572872 | tf_op jit(solution)/shard_map/ppermute | solution.py:8
  355.8 42.4 %copy-start.2 = (bf16[256,512]{1,0:T(8,128)(2,1)S(1)}, bf16[256,512]{1,0:T(8,128)(2,1)}, u32[]{:S(2)}) copy-start(bf16[256,512]{1,0:T(8,128)(2,1)} %param.6) | copy-start | bytes 786436
  355.8 39.1 %collective-permute-start.4 = (f32[256,512]{0,1:T(8,128)S(1)}, f32[256,512]{0,1:T(8,128)S(1)}, u32[]{:S(2)}, u32[]{:S(2)}) collective-permute-start(f32[256,512]{0,1:T(8,128)S(1)} %convolution_bitcast_fusion.3), channel_id=1, source_target_pairs={{0,128},{4,132},{8,136},{12,140},{16,144},{20,148},{24,152},{28,15... | collective-permute-start | bytes 1572872 | tf_op jit(solution)/shard_map/ppermute | solution.py:8
  395.6 17.0 %copy-start.3 = (bf16[256,256]{1,0:T(8,128)(2,1)S(1)}, bf16[256,256]{1,0:T(8,128)(2,1)}, u32[]{:S(2)}) copy-start(bf16[256,256]{1,0:T(8,128)(2,1)} %param.7) | copy-start | bytes 393220
  396.2 14.6 %collective-permute-start.5 = (f32[256,512]{1,0:T(8,128)S(1)}, f32[256,512]{1,0:T(8,128)}, u32[]{:S(2)}, u32[]{:S(2)}) collective-permute-start(f32[256,512]{1,0:T(8,128)S(1)} %convolution_bitcast_fusion.1), channel_id=1, source_target_pairs={{0,64},{4,68},{8,72},{12,76},{16,80},{20,84},{24,88},{28,92},{32,9... | collective-permute-start | bytes 1572872 | tf_op jit(solution)/shard_map/ppermute | solution.py:8
Sparse Core Ops, SparseCore 0:
  9.7 57.0 all-reduce.2
  142.9 189.6 all-reduce.4
where the time goes:
time: 421 us
  waiting for transfers between devices  349 us (83%)
  starting transfers between devices  40.2 us (10%)
  matrix products  15.3 us (4%)
  between operations  14.3 us (3%)
    psum x1, waiting for transfers between devices, local(): root_sum = lax.psum(times_left(project, upward), 'box')  190 us
    ppermute x6, waiting for transfers between devices, swapped(): lax.ppermute(value, axis, [(i, i ^ 1 << stride) for i in range(lax.axis_s...  102 us
    psum x1, waiting for transfers between devices, local(): skeleton = lax.psum(leaf_term, 'sub')  57.3 us
    ppermute x6, starting transfers between devices, swapped(): lax.ppermute(value, axis, [(i, i ^ 1 << stride) for i in range(lax.axis_s...  40.1 us
  transfers between devices with their start and end apart: 8, of which 8 were waited for; matrix products, arithmetic and copies ran while one was open for 1% of the time, Pallas kernels for 0%

commit v1 on v0

v1 whole, which is shorter than its diff:
```python
import functools

import jax
import jax.numpy as jnp
from jax import lax
from jax.experimental import pallas as pl
from jax.experimental.pallas import tpu as pltpu
from jax.sharding import PartitionSpec as P

F32 = jnp.float32
BF16 = jnp.bfloat16
MESH = pl.DeviceIdType.MESH
CHUNKS = 2
NN = (((1,), (0,)), ((), ()))
NT = (((1,), (1,)), ((), ()))


def halves(value):
    high = value.astype(BF16)
    return high, (value - high.astype(F32)).astype(BF16)


def dot(left, right, dims):
    return lax.dot_general(left, right, dims, preferred_element_type=F32)


def dot_split(value, high, low, dims):
    rows = value.shape[0]
    value_high, value_low = halves(value)
    both = dot(jnp.concatenate([value_high, value_low], axis=0), high, dims)
    return both[:rows] + (both[rows:] + dot(value_high, low, dims))


def kernel(
    n_y, n_z, n_sub, levels,
    rhs_hbm, interp_hbm, count_ref, butterfly_hbm, project_hbm, inverse_hbm, out_hbm,
    rhs, interp, interp_t, butterfly, project, inverse,
    weight_high, weight_low, project_high, project_low, inverse_high, inverse_low,
    leaf, leaf_in, up, up_in, down_out, down_in,
    sweep, sweep_out, sweep_in, root_map,
    root_part, root_core, root_y, root_mine, root_z, root_piece, root_all,
    back, out,
    load_sem, out_sem, leaf_sem, up_sem, down_sem, sweep_sem, map_sem, core_sem, y_sem, z_sem, spread_sem,
    swap_sem, back_sem,
):
    width = interp.shape[0]
    slice_cols = leaf.shape[1]
    half = slice_cols // 2
    chunk = slice_cols // CHUNKS
    root_rows = width // n_sub
    piece = half // n_y

    box = lax.axis_index("box")
    x = lax.axis_index("sub")
    core = box % 2
    y = (box // 2) % n_y
    z = box // (2 * n_y)

    def at_x(k):
        return (box, (x + k) % n_sub)

    def at_y(k):
        return (z * 2 * n_y + ((y + k) % n_y) * 2 + core, x)

    def at_z(k):
        return (((z + k) % n_z) * 2 * n_y + y * 2 + core, x)

    def sibling(level):
        bit = 2 ** level
        return (box + (1 - 2 * ((z // bit) % 2)) * bit * 2 * n_y, x)

    other_core = (box + 1 - 2 * core, x)

    def send(source, target, sems, index, device):
        copy = pltpu.make_async_remote_copy(
            src_ref=source, dst_ref=target, send_sem=sems.at[0, index], recv_sem=sems.at[1, index],
            device_id=device, device_id_type=MESH,
        )
        copy.start()
        started.append(copy)
        return copy

    started = []

    loads = []
    for source, target in (
        (project_hbm, project), (butterfly_hbm.at[2], butterfly.at[2]), (interp_hbm, interp), (rhs_hbm, rhs),
        (butterfly_hbm.at[1], butterfly.at[1]),
        (butterfly_hbm.at[0], butterfly.at[0]), (inverse_hbm, inverse),
    ):
        load = pltpu.make_async_copy(source, target, load_sem.at[len(loads)])
        load.start()
        loads.append(load)

    barrier = pltpu.get_barrier_semaphore()
    peers = ([at_x(k) for k in range(1, n_sub)] + [at_y(k) for k in range(1, n_y)]
             + [at_z(k) for k in range(1, n_z)] + [other_core])
    for peer in peers:
        pl.semaphore_signal(barrier, inc=1, device_id=peer, device_id_type=MESH)

    def split_level(level):
        high, low = halves(butterfly[level])
        weight_high[level] = high
        weight_low[level] = low

    def own(value, level, dims):
        return dot_split(value, weight_high[level, :, :width], weight_low[level, :, :width], dims)

    def cross(value, level, dims):
        return dot_split(value, weight_high[level, :, width:], weight_low[level, :, width:], dims)

    loads[0].wait()
    loads[1].wait()
    split_level(levels - 1)
    sweep[levels] = project[pl.ds(pl.multiple_of(x * root_rows, root_rows), root_rows), :]
    sweep_out[levels - 1] = cross(sweep[levels], levels - 1, NN)

    pl.semaphore_wait(barrier, len(peers))

    sweep_copies = {}

    def sweep_send(level):
        sweep_copies[level] = send(
            sweep_out.at[level], sweep_in.at[level], sweep_sem, level, sibling(level))

    def sweep_take(level):
        sweep[level] = own(sweep[level + 1], level, NN)
        sweep_copies[level].wait_recv()
        sweep[level] = sweep[level] + sweep_in[level]
        if level > 0:
            sweep_out[level - 1] = cross(sweep[level], level - 1, NN)
            sweep_send(level - 1)

    sweep_send(levels - 1)

    loads[2].wait()
    loads[3].wait()
    interp_value = interp[...]
    leaf_order = sorted(range(n_sub), key=lambda k: (k == 0, -min(k, n_sub - k)))
    leaf_copies = {}
    turned = {}
    for k in leaf_order:
        columns = pl.ds(pl.multiple_of(((x + k) % n_sub) * slice_cols, slice_cols), slice_cols)
        turned[k] = rhs[:, columns].T
    for j in range(CHUNKS):
        rows = pl.ds(j * chunk, chunk)
        for k in leaf_order[:-1]:
            leaf[k, rows] = dot(turned[k][j * chunk:(j + 1) * chunk], interp_value, NT)
            leaf_copies[j, k] = send(leaf.at[k, rows], leaf_in.at[k, rows], leaf_sem, j * n_sub + k, at_x(k))
    leaf[0] = dot(turned[0], interp_value, NT)

    for position, level in ((4, 1), (5, 0)):
        loads[position].wait()
        split_level(level)
    project_high[...], project_low[...] = halves(project[...])
    loads[6].wait()
    inverse_high[...], inverse_low[...] = halves(inverse[...])
    interp_t[...] = interp_value.T
    live = lax.broadcasted_iota(jnp.int32, (chunk, width), 1) < count_ref[0]

    up_copies = {}
    up_own = {}

    def up_send(level, j):
        rows = pl.ds(j * chunk, chunk)
        up_copies[level, j] = send(
            up.at[level, rows], up_in.at[level, rows], up_sem, level * CHUNKS + j, sibling(level))

    def up_start(j):
        rows = pl.ds(j * chunk, chunk)
        total = leaf[0, rows]
        for k in leaf_order[:-1][::-1]:
            leaf_copies[j, k].wait_recv()
            total = total + leaf_in[k, rows]
        up[0, rows] = jnp.where(live, total, 0.0)
        up_send(0, j)
        up_own[j] = own(up[0, rows], 0, NT)

    def up_step(level, j):
        rows = pl.ds(j * chunk, chunk)
        up_copies[level, j].wait_recv()
        up[level + 1, rows] = up_own[j] + cross(up_in[level, rows], level, NT)
        if level + 1 < levels:
            up_send(level + 1, j)
            up_own[j] = own(up[level + 1, rows], level + 1, NT)

    down_copies = {}
    down_own = {}

    def down_send(value, level, j):
        rows = pl.ds(j * chunk, chunk)
        down_out[level, rows] = cross(value, level, NN).astype(BF16)
        down_copies[level, j] = send(
            down_out.at[level, rows], down_in.at[level, rows], down_sem, level * CHUNKS + j, sibling(level))
        down_own[j] = own(value, level, NN)

    def down_take(level, j):
        rows = pl.ds(j * chunk, chunk)
        down_copies[level, j].wait_recv()
        value = down_own[j] + down_in[level, rows].astype(F32)
        if level > 0:
            down_send(value, level - 1, j)
        else:
            leaf[0, rows] = value

    sweep_take(2)
    for j in range(CHUNKS):
        up_start(j)
    sweep_take(1)
    for j in range(CHUNKS):
        up_step(0, j)
    sweep_take(0)
    my_rows = pl.ds(pl.multiple_of(x * root_rows, root_rows), root_rows)
    root_map[my_rows] = sweep[0]
    map_copies = [
        send(sweep.at[0], root_map.at[my_rows], map_sem, k, at_x(k)) for k in range(1, n_sub)]
    for j in range(CHUNKS):
        up_step(1, j)
    for j in range(CHUNKS):
        rows = pl.ds(j * chunk, chunk)
        up_step(2, j)
        value = up[levels, rows]
        root_part[rows] = dot_split(value, project_high[...], project_low[...], NT)
        if j == CHUNKS - 1:
            my_half = pl.ds(pl.multiple_of(core * half, half), half)
            other_half = pl.ds(pl.multiple_of((1 - core) * half, half), half)
            core_copy = send(root_part.at[other_half], root_core, core_sem, 0, other_core)
        down_send(value, levels - 1, j)

    def piece_of(k):
        return pl.ds(pl.multiple_of(((y + k) % n_y) * piece, piece), piece)

    def down_part(level, part):
        for j in range(part * CHUNKS // 2, (part + 1) * CHUNKS // 2):
            down_take(level, j)

    core_copy.wait_recv()
    root_core[...] = root_core[...] + root_part[my_half]
    y_copies = [send(root_core.at[piece_of(k)], root_y.at[k], y_sem, k, at_y(k)) for k in range(1, n_y)]
    down_part(2, 0)
    total = root_core[piece_of(0)]
    for k, copy in enumerate(y_copies, 1):
        copy.wait_recv()
        total = total + root_y[k]
    root_mine[...] = total
    z_copies = [send(root_mine, root_z.at[k], z_sem, k, at_z(k)) for k in range(1, n_z)]
    down_part(2, 1)
    for k, copy in enumerate(z_copies, 1):
        copy.wait_recv()
        total = total + root_z[k]
    padded = jnp.concatenate([total, jnp.zeros_like(total)], axis=0)
    solved = dot_split(padded, inverse_high[...], inverse_low[...], NT)[:piece]
    root_piece[...] = solved
    mine = pl.ds(pl.multiple_of(core * half + y * piece, piece), piece)
    root_all[mine] = solved
    spread_copies = [
        send(root_piece, root_all.at[mine], spread_sem, k, at_y(k)) for k in range(1, n_y)]
    down_part(1, 0)
    for copy in spread_copies:
        copy.wait_recv()
    swap_copy = send(root_all.at[my_half], root_all.at[my_half], swap_sem, 0, other_core)
    down_part(1, 1)
    for copy in map_copies:
        copy.wait_recv()
    map_high, map_low = halves(root_map[...])
    swap_copy.wait_recv()
    root_term = dot_split(root_all[...], map_high, map_low, NN)

    back_copies = {}
    for j in range(CHUNKS):
        rows = pl.ds(j * chunk, chunk)
        down_take(0, j)
        value = leaf[0, rows] - root_term[j * chunk:(j + 1) * chunk]
        spot = pl.ds(pl.multiple_of(x * slice_cols + j * chunk, chunk), chunk)
        back[spot] = jnp.where(live, value, 0.0).astype(BF16)
        for k in leaf_order[:-1]:
            back_copies[j, k] = send(back.at[spot], back.at[spot], back_sem, j * n_sub + k, at_x(k))

    out_copies = []
    for k in (0, *leaf_order[:-1][::-1]):
        columns = pl.ds(pl.multiple_of(((x + n_sub - k) % n_sub) * slice_cols, slice_cols), slice_cols)
        if k:
            for j in range(CHUNKS):
                back_copies[j, k].wait_recv()
        out[:, columns] = rhs[:, columns].astype(F32) - dot(interp_t[...], back[columns], NT)
        copy = pltpu.make_async_copy(out.at[:, columns], out_hbm.at[:, columns], out_sem.at[k])
        copy.start()
        out_copies.append(copy)

    for copy in started:
        copy.wait_send()
    for copy in out_copies:
        copy.wait()


def local(n_y, n_z, n_sub, rhs_points, interp, skel_count, butterfly, project, root_inverse):
    points, columns = rhs_points.shape
    width = interp.shape[0]
    levels = butterfly.shape[0]
    slice_cols = columns // n_sub
    half = slice_cols // 2
    piece = half // n_y
    root_rows = width // n_sub
    vmem = pltpu.VMEM
    pair = lambda count: pltpu.SemaphoreType.DMA((2, count))
    scratch = [
        vmem((points, columns), BF16), vmem((width, points), BF16), vmem((points, width), BF16),
        vmem(butterfly.shape, F32), vmem((width, width), F32), vmem((width, width), F32),
        vmem(butterfly.shape, BF16), vmem(butterfly.shape, BF16),
        vmem((width, width), BF16), vmem((width, width), BF16), vmem((width, width), BF16), vmem((width, width), BF16),
        vmem((n_sub, slice_cols, width), F32), vmem((n_sub, slice_cols, width), F32),
        vmem((levels + 1, slice_cols, width), F32), vmem((levels, slice_cols, width), F32),
        vmem((levels, slice_cols, width), BF16), vmem((levels, slice_cols, width), BF16),
        vmem((levels + 1, root_rows, width), F32), vmem((levels, root_rows, width), F32),
        vmem((levels, root_rows, width), F32), vmem((width, width), F32),
        vmem((slice_cols, width), F32), vmem((half, width), F32), vmem((n_y, piece, width), F32),
        vmem((piece, width), F32), vmem((n_z, piece, width), F32), vmem((piece, width), F32),
        vmem((slice_cols, width), F32),
        vmem((columns, width), BF16), vmem((points, columns), F32),
        pltpu.SemaphoreType.DMA((7,)), pltpu.SemaphoreType.DMA((n_sub,)),
        pair(CHUNKS * n_sub), pair(levels * CHUNKS), pair(levels * CHUNKS), pair(levels), pair(n_sub),
        pair(1), pair(n_y), pair(n_z), pair(n_y), pair(1), pair(CHUNKS * n_sub),
    ]
    anywhere = pl.BlockSpec(memory_space=pl.ANY)
    return pl.pallas_call(
        functools.partial(kernel, n_y, n_z, n_sub, levels),
        out_shape=jax.ShapeDtypeStruct((points, columns), F32),
        in_specs=[anywhere, anywhere, pl.BlockSpec(memory_space=pltpu.SMEM), anywhere, anywhere, anywhere],
        out_specs=anywhere,
        scratch_shapes=scratch,
        compiler_params=pltpu.CompilerParams(
            collective_id=0, has_side_effects=True, vmem_limit_bytes=62 * 2**20),
    )(rhs_points, interp, skel_count, butterfly, project, root_inverse)


def solution(mesh):
    n_box, n_sub = mesh.shape["box"], mesh.shape["sub"]
    n_z = 8
    n_y = n_box // (2 * n_z)
    in_specs = (
        P(("box", "sub"), None),
        P(("box", "sub"), None),
        P("box"),
        P(None, "box", None),
        P("box", None),
        P(),
    )
    out_specs = P(("box", "sub"), None)
    return jax.shard_map(
        functools.partial(local, n_y, n_z, n_sub),
        mesh=mesh, in_specs=in_specs, out_specs=out_specs, check_vma=False)
```

time: 421 us -> 72.1 us (0.17)
  waiting for transfers between devices: 349 us -> 0 us
  Pallas kernels: 0 us -> 69.4 us
  starting transfers between devices: 40.2 us -> 0 us
  matrix products: 15.3 us -> 0 us
  between operations: 14.3 us -> 0.66 us
    psum x2 -> x0, waiting for transfers between devices: 247 us -> none  [the longest x1 190 us: local(): root_sum = lax.psum(times_left(project, upward), 'box')]
    ppermute x6 -> x0, waiting for transfers between devices: 102 us -> none  [swapped(): lax.ppermute(value, axis, [(i, i ^ 1 << stride) for i in range(lax.axis_s...]
    pallas_call x0 -> x1, Pallas kernels: none -> 69.4 us  [local(): pl.pallas_call(functools.partial(kernel, n_y, n_z, n_sub, levels), out_sh...]
    ppermute x6 -> x0, starting transfers between devices: 40.1 us -> none  [swapped(): lax.ppermute(value, axis, [(i, i ^ 1 << stride) for i in range(lax.axis_s...]
    dot_general x17 -> x0, matrix products: 15.3 us -> none  [the longest x8 7.58 us: times_left(): jnp.dot(matrix, block_rows, precision=lax.Precision.HIGHEST, preferred_el...]
  transfers between devices with their start and end apart: 8 -> 0, of which waited for: 8 -> 0; matrix products, arithmetic and copies ran while one was open for 1% -> 0% of each run, Pallas kernels for 0% -> 0%
where the time goes in v1:
time: 72.1 us; the launch traced here: 72 us
  Pallas kernels  69.4 us (96%)
  local copies, waits for them, and re-layouts  1.87 us (3%)
    pallas_call x1, Pallas kernels, local(): pl.pallas_call(functools.partial(kernel, n_y, n_z, n_sub, levels), out_sh...  69.4 us
    unnamed x1, local copies, waits for them, and re-layouts  1.87 us

profile of v1, /device:TPU:1, one launch (start us, length us, event | category | flops | bytes accessed | tf_op | source)
XLA Modules:
  0.0 72.0 jit_solution(2764608583207499028)
XLA Ops:
  0.7 69.4 %shard_map.64 = f32[256,512]{1,0:T(8,128)} custom-call(bf16[256,512]{1,0:T(8,128)(2,1)} %rhs_hbm.1, bf16[256,256]{1,0:T(8,128)(2,1)} %interp_hbm.1, s32[1]{0:T(128)S(6)} %copy.8.count_ref, f32[3,256,512]{2,1,0:T(8,128)} %butterfly_hbm.1, f32[256,256]{1,0:T(8,128)} %project_hbm.1, f32[256,256]{1,0:T(8,128)} %inverse_hbm.1), custom_call_target="tpu_custom_call" | custom-call | tf_op jit(solution)/shard_map/pallas_call | solution.py:325
  70.1 1.9 %copy.9 = f32[256,512]{1,0:T(8,128)} copy(f32[256,512]{1,0:T(8,128)} %shard_map.64) | data formatting | bytes 1048576

commit v2 on v1

--- a/solution.py
+++ b/solution.py
@@ -34,13 +34,13 @@
 def kernel(
     n_y, n_z, n_sub, levels,
     rhs_hbm, interp_hbm, count_ref, butterfly_hbm, project_hbm, inverse_hbm, out_hbm,
-    rhs, interp, interp_t, butterfly, project, inverse,
-    weight_high, weight_low, project_high, project_low, inverse_high, inverse_low,
+    rhs, interp, interp_t, butterfly, inverse,
+    weight_high, weight_low, inverse_high, inverse_low,
     leaf, leaf_in, up, up_in, down_out, down_in,
-    sweep, sweep_out, sweep_in, root_map,
+    sweep, sweep_out, sweep_in, step_map, root_map,
     root_part, root_core, root_y, root_mine, root_z, root_piece, root_all,
     back, out,
-    load_sem, out_sem, leaf_sem, up_sem, down_sem, sweep_sem, map_sem, core_sem, y_sem, z_sem, spread_sem,
+    load_sem, out_sem, leaf_sem, up_sem, down_sem, sweep_sem, step_sem, map_sem, core_sem, y_sem, z_sem, spread_sem,
     swap_sem, back_sem,
 ):
     width = interp.shape[0]
@@ -82,11 +82,12 @@
 
     started = []
 
+    my_rows = pl.ds(pl.multiple_of(x * root_rows, root_rows), root_rows)
     loads = []
     for source, target in (
-        (project_hbm, project), (butterfly_hbm.at[2], butterfly.at[2]), (interp_hbm, interp), (rhs_hbm, rhs),
-        (butterfly_hbm.at[1], butterfly.at[1]),
-        (butterfly_hbm.at[0], butterfly.at[0]), (inverse_hbm, inverse),
+        (interp_hbm, interp), (rhs_hbm, rhs), (project_hbm.at[my_rows], sweep.at[levels]),
+        (butterfly_hbm.at[2], butterfly.at[2]), (butterfly_hbm.at[0], butterfly.at[0]),
+        (butterfly_hbm.at[1], butterfly.at[1]), (inverse_hbm, inverse),
     ):
         load = pltpu.make_async_copy(source, target, load_sem.at[len(loads)])
         load.start()
@@ -98,6 +99,22 @@
     for peer in peers:
         pl.semaphore_signal(barrier, inc=1, device_id=peer, device_id_type=MESH)
 
+    leaf_order = sorted(range(n_sub), key=lambda k: (k == 0, -min(k, n_sub - k)))
+    loads[0].wait()
+    loads[1].wait()
+    interp_value = interp[...]
+    for k in leaf_order:
+        columns = pl.ds(pl.multiple_of(((x + k) % n_sub) * slice_cols, slice_cols), slice_cols)
+        leaf[k] = dot(rhs[:, columns].T, interp_value, NT)
+
+    pl.semaphore_wait(barrier, len(peers))
+
+    leaf_copies = {}
+    for j in range(CHUNKS):
+        rows = pl.ds(j * chunk, chunk)
+        for k in leaf_order[:-1]:
+            leaf_copies[j, k] = send(leaf.at[k, rows], leaf_in.at[k, rows], leaf_sem, j * n_sub + k, at_x(k))
+
     def split_level(level):
         high, low = halves(butterfly[level])
         weight_high[level] = high
@@ -109,50 +126,31 @@
     def cross(value, level, dims):
         return dot_split(value, weight_high[level, :, width:], weight_low[level, :, width:], dims)
 
-    loads[0].wait()
-    loads[1].wait()
-    split_level(levels - 1)
-    sweep[levels] = project[pl.ds(pl.multiple_of(x * root_rows, root_rows), root_rows), :]
-    sweep_out[levels - 1] = cross(sweep[levels], levels - 1, NN)
-
-    pl.semaphore_wait(barrier, len(peers))
-
     sweep_copies = {}
 
     def sweep_send(level):
+        sweep_out[level] = cross(sweep[level + 1], level, NN)
         sweep_copies[level] = send(
             sweep_out.at[level], sweep_in.at[level], sweep_sem, level, sibling(level))
+        sweep[level] = own(sweep[level + 1], level, NN)
 
     def sweep_take(level):
-        sweep[level] = own(sweep[level + 1], level, NN)
         sweep_copies[level].wait_recv()
         sweep[level] = sweep[level] + sweep_in[level]
         if level > 0:
-            sweep_out[level - 1] = cross(sweep[level], level - 1, NN)
             sweep_send(level - 1)
 
-    sweep_send(levels - 1)
+    def gather(level, target, sems):
+        target[my_rows] = sweep[level]
+        return [send(sweep.at[level], target.at[my_rows], sems, k, at_x(k)) for k in range(1, n_sub)]
 
     loads[2].wait()
     loads[3].wait()
-    interp_value = interp[...]
-    leaf_order = sorted(range(n_sub), key=lambda k: (k == 0, -min(k, n_sub - k)))
-    leaf_copies = {}
-    turned = {}
-    for k in leaf_order:
-        columns = pl.ds(pl.multiple_of(((x + k) % n_sub) * slice_cols, slice_cols), slice_cols)
-        turned[k] = rhs[:, columns].T
-    for j in range(CHUNKS):
-        rows = pl.ds(j * chunk, chunk)
-        for k in leaf_order[:-1]:
-            leaf[k, rows] = dot(turned[k][j * chunk:(j + 1) * chunk], interp_value, NT)
-            leaf_copies[j, k] = send(leaf.at[k, rows], leaf_in.at[k, rows], leaf_sem, j * n_sub + k, at_x(k))
-    leaf[0] = dot(turned[0], interp_value, NT)
-
-    for position, level in ((4, 1), (5, 0)):
+    split_level(2)
+    sweep_send(levels - 1)
+    for position, level in ((4, 0), (5, 1)):
         loads[position].wait()
         split_level(level)
-    project_high[...], project_low[...] = halves(project[...])
     loads[6].wait()
     inverse_high[...], inverse_low[...] = halves(inverse[...])
     interp_t[...] = interp_value.T
@@ -203,48 +201,50 @@
         else:
             leaf[0, rows] = value
 
-    sweep_take(2)
-    for j in range(CHUNKS):
-        up_start(j)
-    sweep_take(1)
-    for j in range(CHUNKS):
-        up_step(0, j)
-    sweep_take(0)
-    my_rows = pl.ds(pl.multiple_of(x * root_rows, root_rows), root_rows)
-    root_map[my_rows] = sweep[0]
-    map_copies = [
-        send(sweep.at[0], root_map.at[my_rows], map_sem, k, at_x(k)) for k in range(1, n_sub)]
-    for j in range(CHUNKS):
-        up_step(1, j)
-    for j in range(CHUNKS):
-        rows = pl.ds(j * chunk, chunk)
-        up_step(2, j)
-        value = up[levels, rows]
-        root_part[rows] = dot_split(value, project_high[...], project_low[...], NT)
-        if j == CHUNKS - 1:
-            my_half = pl.ds(pl.multiple_of(core * half, half), half)
-            other_half = pl.ds(pl.multiple_of((1 - core) * half, half), half)
-            core_copy = send(root_part.at[other_half], root_core, core_sem, 0, other_core)
-        down_send(value, levels - 1, j)
-
-    def piece_of(k):
-        return pl.ds(pl.multiple_of(((y + k) % n_y) * piece, piece), piece)
+    def up_part(level, part):
+        for j in range(part * CHUNKS // 2, (part + 1) * CHUNKS // 2):
+            up_step(level, j)
+            if level == levels - 1:
+                down_send(up[levels, pl.ds(j * chunk, chunk)], levels - 1, j)
 
     def down_part(level, part):
         for j in range(part * CHUNKS // 2, (part + 1) * CHUNKS // 2):
             down_take(level, j)
 
+    for j in range(CHUNKS):
+        up_start(j)
+    sweep_take(2)
+    step_copies = gather(2, step_map, step_sem)
+    up_part(0, 0)
+    up_part(0, 1)
+    up_part(1, 0)
+    sweep_take(1)
+    up_part(1, 1)
+
+    for copy in step_copies:
+        copy.wait_recv()
+    step_high, step_low = halves(step_map[...])
+    root_part[...] = dot_split(up[levels - 1], step_high, step_low, NT)
+    my_half = pl.ds(pl.multiple_of(core * half, half), half)
+    other_half = pl.ds(pl.multiple_of((1 - core) * half, half), half)
+    core_copy = send(root_part.at[other_half], root_core, core_sem, 0, other_core)
+    sweep_take(0)
+    map_copies = gather(0, root_map, map_sem)
+
+    def piece_of(k):
+        return pl.ds(pl.multiple_of(((y + k) % n_y) * piece, piece), piece)
+
     core_copy.wait_recv()
     root_core[...] = root_core[...] + root_part[my_half]
     y_copies = [send(root_core.at[piece_of(k)], root_y.at[k], y_sem, k, at_y(k)) for k in range(1, n_y)]
-    down_part(2, 0)
+    up_part(2, 0)
     total = root_core[piece_of(0)]
     for k, copy in enumerate(y_copies, 1):
         copy.wait_recv()
         total = total + root_y[k]
     root_mine[...] = total
     z_copies = [send(root_mine, root_z.at[k], z_sem, k, at_z(k)) for k in range(1, n_z)]
-    down_part(2, 1)
+    up_part(2, 1)
     for k, copy in enumerate(z_copies, 1):
         copy.wait_recv()
         total = total + root_z[k]
@@ -255,16 +255,18 @@
     root_all[mine] = solved
     spread_copies = [
         send(root_piece, root_all.at[mine], spread_sem, k, at_y(k)) for k in range(1, n_y)]
+    down_part(2, 0)
+    down_part(2, 1)
+    for copy in spread_copies:
+        copy.wait_recv()
+    swap_copy = send(root_all.at[my_half], root_all.at[my_half], swap_sem, 0, other_core)
     down_part(1, 0)
-    for copy in spread_copies:
-        copy.wait_recv()
-    swap_copy = send(root_all.at[my_half], root_all.at[my_half], swap_sem, 0, other_core)
-    down_part(1, 1)
     for copy in map_copies:
         copy.wait_recv()
     map_high, map_low = halves(root_map[...])
     swap_copy.wait_recv()
     root_term = dot_split(root_all[...], map_high, map_low, NN)
+    down_part(1, 1)
 
     back_copies = {}
     for j in range(CHUNKS):
@@ -305,28 +307,28 @@
     pair = lambda count: pltpu.SemaphoreType.DMA((2, count))
     scratch = [
         vmem((points, columns), BF16), vmem((width, points), BF16), vmem((points, width), BF16),
-        vmem(butterfly.shape, F32), vmem((width, width), F32), vmem((width, width), F32),
+        vmem(butterfly.shape, F32), vmem((width, width), F32),
         vmem(butterfly.shape, BF16), vmem(butterfly.shape, BF16),
-        vmem((width, width), BF16), vmem((width, width), BF16), vmem((width, width), BF16), vmem((width, width), BF16),
+        vmem((width, width), BF16), vmem((width, width), BF16),
         vmem((n_sub, slice_cols, width), F32), vmem((n_sub, slice_cols, width), F32),
         vmem((levels + 1, slice_cols, width), F32), vmem((levels, slice_cols, width), F32),
         vmem((levels, slice_cols, width), BF16), vmem((levels, slice_cols, width), BF16),
         vmem((levels + 1, root_rows, width), F32), vmem((levels, root_rows, width), F32),
-        vmem((levels, root_rows, width), F32), vmem((width, width), F32),
+        vmem((levels, root_rows, width), F32), vmem((width, width), F32), vmem((width, width), F32),
         vmem((slice_cols, width), F32), vmem((half, width), F32), vmem((n_y, piece, width), F32),
         vmem((piece, width), F32), vmem((n_z, piece, width), F32), vmem((piece, width), F32),
         vmem((slice_cols, width), F32),
         vmem((columns, width), BF16), vmem((points, columns), F32),
         pltpu.SemaphoreType.DMA((7,)), pltpu.SemaphoreType.DMA((n_sub,)),
-        pair(CHUNKS * n_sub), pair(levels * CHUNKS), pair(levels * CHUNKS), pair(levels), pair(n_sub),
+        pair(CHUNKS * n_sub), pair(levels * CHUNKS), pair(levels * CHUNKS), pair(levels), pair(n_sub), pair(n_sub),
         pair(1), pair(n_y), pair(n_z), pair(n_y), pair(1), pair(CHUNKS * n_sub),
     ]
-    anywhere = pl.BlockSpec(memory_space=pl.ANY)
+    hbm = pl.BlockSpec(memory_space=pl.ANY)
     return pl.pallas_call(
         functools.partial(kernel, n_y, n_z, n_sub, levels),
         out_shape=jax.ShapeDtypeStruct((points, columns), F32),
-        in_specs=[anywhere, anywhere, pl.BlockSpec(memory_space=pltpu.SMEM), anywhere, anywhere, anywhere],
-        out_specs=anywhere,
+        in_specs=[hbm, hbm, pl.BlockSpec(memory_space=pltpu.SMEM), hbm, hbm, hbm],
+        out_specs=pl.BlockSpec(memory_space=pl.ANY),
         scratch_shapes=scratch,
         compiler_params=pltpu.CompilerParams(
             collective_id=0, has_side_effects=True, vmem_limit_bytes=62 * 2**20),

time: 72.1 us -> 66.3 us (0.920)
  Pallas kernels: 69.4 us -> 63.6 us
    pallas_call x1, Pallas kernels: 69.4 us -> 63.6 us  [local(): pl.pallas_call(functools.partial(kernel, n_y, n_z, n_sub, levels), out_sh...]
where the time goes in v2:
time: 66.3 us; the launch traced here: 66.2 us
  Pallas kernels  63.6 us (96%)
  local copies, waits for them, and re-layouts  1.87 us (3%)
    pallas_call x1, Pallas kernels, local(): pl.pallas_call(functools.partial(kernel, n_y, n_z, n_sub, levels), out_sh...  63.6 us
    unnamed x1, local copies, waits for them, and re-layouts  1.87 us

profile of v2, /device:TPU:1, one launch (start us, length us, event | category | flops | bytes accessed | tf_op | source)
XLA Modules:
  0.0 66.2 jit_solution(14267489788219747080)
XLA Ops:
  0.7 63.6 %shard_map.64 = f32[256,512]{1,0:T(8,128)} custom-call(bf16[256,512]{1,0:T(8,128)(2,1)} %rhs_hbm.1, bf16[256,256]{1,0:T(8,128)(2,1)} %interp_hbm.1, s32[1]{0:T(128)S(6)} %copy.8.count_ref, f32[3,256,512]{2,1,0:T(8,128)} %butterfly_hbm.1, f32[256,256]{1,0:T(8,128)} %project_hbm.1, f32[256,256]{1,0:T(8,128)} %inverse_hbm.1), custom_call_target="tpu_custom_call" | custom-call | tf_op jit(solution)/shard_map/pallas_call | solution.py:327
  64.3 1.9 %copy.9 = f32[256,512]{1,0:T(8,128)} copy(f32[256,512]{1,0:T(8,128)} %shard_map.64) | data formatting | bytes 1048576

commit v3 on v2

--- a/solution.py
+++ b/solution.py
@@ -26,6 +26,8 @@
 
 def dot_split(value, high, low, dims):
     rows = value.shape[0]
+    if value.dtype == BF16:
+        return dot(value, high, dims) + dot(value, low, dims)
     value_high, value_low = halves(value)
     both = dot(jnp.concatenate([value_high, value_low], axis=0), high, dims)
     return both[:rows] + (both[rows:] + dot(value_high, low, dims))
@@ -36,11 +38,11 @@
     rhs_hbm, interp_hbm, count_ref, butterfly_hbm, project_hbm, inverse_hbm, out_hbm,
     rhs, interp, interp_t, butterfly, inverse,
     weight_high, weight_low, inverse_high, inverse_low,
-    leaf, leaf_in, up, up_in, down_out, down_in,
-    sweep, sweep_out, sweep_in, step_map, root_map,
+    leaf, leaf_in, up, up_wide_in, up_out, up_in, down_wide_out, down_wide_in, down_out, down_in,
+    sweep, sweep_out, sweep_in, root_map,
     root_part, root_core, root_y, root_mine, root_z, root_piece, root_all,
     back, out,
-    load_sem, out_sem, leaf_sem, up_sem, down_sem, sweep_sem, step_sem, map_sem, core_sem, y_sem, z_sem, spread_sem,
+    load_sem, out_sem, leaf_sem, up_sem, down_sem, sweep_sem, map_sem, core_sem, y_sem, z_sem, spread_sem,
     swap_sem, back_sem,
 ):
     width = interp.shape[0]
@@ -85,7 +87,7 @@
     my_rows = pl.ds(pl.multiple_of(x * root_rows, root_rows), root_rows)
     loads = []
     for source, target in (
-        (interp_hbm, interp), (rhs_hbm, rhs), (project_hbm.at[my_rows], sweep.at[levels]),
+        (interp_hbm, interp), (rhs_hbm, rhs), (project_hbm.at[my_rows], sweep.at[1]),
         (butterfly_hbm.at[2], butterfly.at[2]), (butterfly_hbm.at[0], butterfly.at[0]),
         (butterfly_hbm.at[1], butterfly.at[1]), (inverse_hbm, inverse),
     ):
@@ -126,28 +128,12 @@
     def cross(value, level, dims):
         return dot_split(value, weight_high[level, :, width:], weight_low[level, :, width:], dims)
 
-    sweep_copies = {}
-
-    def sweep_send(level):
-        sweep_out[level] = cross(sweep[level + 1], level, NN)
-        sweep_copies[level] = send(
-            sweep_out.at[level], sweep_in.at[level], sweep_sem, level, sibling(level))
-        sweep[level] = own(sweep[level + 1], level, NN)
-
-    def sweep_take(level):
-        sweep_copies[level].wait_recv()
-        sweep[level] = sweep[level] + sweep_in[level]
-        if level > 0:
-            sweep_send(level - 1)
-
-    def gather(level, target, sems):
-        target[my_rows] = sweep[level]
-        return [send(sweep.at[level], target.at[my_rows], sems, k, at_x(k)) for k in range(1, n_sub)]
-
     loads[2].wait()
     loads[3].wait()
     split_level(2)
-    sweep_send(levels - 1)
+    sweep_out[...] = cross(sweep[1], levels - 1, NN)
+    sweep_copy = send(sweep_out, sweep_in, sweep_sem, 0, sibling(levels - 1))
+    sweep[0] = own(sweep[1], levels - 1, NN)
     for position, level in ((4, 0), (5, 1)):
         loads[position].wait()
         split_level(level)
@@ -161,8 +147,13 @@
 
     def up_send(level, j):
         rows = pl.ds(j * chunk, chunk)
-        up_copies[level, j] = send(
-            up.at[level, rows], up_in.at[level, rows], up_sem, level * CHUNKS + j, sibling(level))
+        if level == 0:
+            source, target = up.at[0, rows], up_wide_in.at[rows]
+        else:
+            up_out[level, rows] = up[level, rows].astype(BF16)
+            source, target = up_out.at[level, rows], up_in.at[level, rows]
+        up_copies[level, j] = send(source, target, up_sem, level * CHUNKS + j, sibling(level))
+        up_own[j] = own(up[level, rows], level, NT)
 
     def up_start(j):
         rows = pl.ds(j * chunk, chunk)
@@ -172,64 +163,56 @@
             total = total + leaf_in[k, rows]
         up[0, rows] = jnp.where(live, total, 0.0)
         up_send(0, j)
-        up_own[j] = own(up[0, rows], 0, NT)
 
     def up_step(level, j):
         rows = pl.ds(j * chunk, chunk)
         up_copies[level, j].wait_recv()
-        up[level + 1, rows] = up_own[j] + cross(up_in[level, rows], level, NT)
+        arrived = up_in[level, rows] if level else up_wide_in[rows]
+        up[level + 1, rows] = up_own[j] + cross(arrived, level, NT)
         if level + 1 < levels:
             up_send(level + 1, j)
-            up_own[j] = own(up[level + 1, rows], level + 1, NT)
+        else:
+            down_send(up[levels, rows], level, j)
 
     down_copies = {}
     down_own = {}
 
     def down_send(value, level, j):
         rows = pl.ds(j * chunk, chunk)
-        down_out[level, rows] = cross(value, level, NN).astype(BF16)
-        down_copies[level, j] = send(
-            down_out.at[level, rows], down_in.at[level, rows], down_sem, level * CHUNKS + j, sibling(level))
+        if level == 0:
+            down_wide_out[rows] = cross(value, level, NN)
+            source, target = down_wide_out.at[rows], down_wide_in.at[rows]
+        else:
+            down_out[level, rows] = cross(value, level, NN).astype(BF16)
+            source, target = down_out.at[level, rows], down_in.at[level, rows]
+        down_copies[level, j] = send(source, target, down_sem, level * CHUNKS + j, sibling(level))
         down_own[j] = own(value, level, NN)
 
-    def down_take(level, j):
+    def down_value(level, j):
         rows = pl.ds(j * chunk, chunk)
         down_copies[level, j].wait_recv()
-        value = down_own[j] + down_in[level, rows].astype(F32)
-        if level > 0:
-            down_send(value, level - 1, j)
-        else:
-            leaf[0, rows] = value
-
-    def up_part(level, part):
-        for j in range(part * CHUNKS // 2, (part + 1) * CHUNKS // 2):
-            up_step(level, j)
-            if level == levels - 1:
-                down_send(up[levels, pl.ds(j * chunk, chunk)], levels - 1, j)
-
-    def down_part(level, part):
-        for j in range(part * CHUNKS // 2, (part + 1) * CHUNKS // 2):
-            down_take(level, j)
+        arrived = down_in[level, rows].astype(F32) if level else down_wide_in[rows]
+        return down_own[j] + arrived
 
     for j in range(CHUNKS):
         up_start(j)
-    sweep_take(2)
-    step_copies = gather(2, step_map, step_sem)
-    up_part(0, 0)
-    up_part(0, 1)
-    up_part(1, 0)
-    sweep_take(1)
-    up_part(1, 1)
-
-    for copy in step_copies:
+    sweep_copy.wait_recv()
+    sweep[0] = sweep[0] + sweep_in[...]
+    root_map[my_rows] = sweep[0]
+    map_copies = [send(sweep.at[0], root_map.at[my_rows], map_sem, k, at_x(k)) for k in range(1, n_sub)]
+    for j in range(CHUNKS):
+        up_step(0, j)
+    for copy in map_copies:
         copy.wait_recv()
-    step_high, step_low = halves(step_map[...])
-    root_part[...] = dot_split(up[levels - 1], step_high, step_low, NT)
+    map_high, map_low = halves(root_map[...])
+
     my_half = pl.ds(pl.multiple_of(core * half, half), half)
     other_half = pl.ds(pl.multiple_of((1 - core) * half, half), half)
+    for j in range(CHUNKS):
+        rows = pl.ds(j * chunk, chunk)
+        up_step(1, j)
+        root_part[rows] = dot_split(up[levels - 1, rows], map_high, map_low, NT)
     core_copy = send(root_part.at[other_half], root_core, core_sem, 0, other_core)
-    sweep_take(0)
-    map_copies = gather(0, root_map, map_sem)
 
     def piece_of(k):
         return pl.ds(pl.multiple_of(((y + k) % n_y) * piece, piece), piece)
@@ -237,14 +220,14 @@
     core_copy.wait_recv()
     root_core[...] = root_core[...] + root_part[my_half]
     y_copies = [send(root_core.at[piece_of(k)], root_y.at[k], y_sem, k, at_y(k)) for k in range(1, n_y)]
-    up_part(2, 0)
     total = root_core[piece_of(0)]
     for k, copy in enumerate(y_copies, 1):
         copy.wait_recv()
         total = total + root_y[k]
     root_mine[...] = total
     z_copies = [send(root_mine, root_z.at[k], z_sem, k, at_z(k)) for k in range(1, n_z)]
-    up_part(2, 1)
+    for j in range(CHUNKS):
+        up_step(2, j)
     for k, copy in enumerate(z_copies, 1):
         copy.wait_recv()
         total = total + root_z[k]
@@ -255,24 +238,19 @@
     root_all[mine] = solved
     spread_copies = [
         send(root_piece, root_all.at[mine], spread_sem, k, at_y(k)) for k in range(1, n_y)]
-    down_part(2, 0)
-    down_part(2, 1)
     for copy in spread_copies:
         copy.wait_recv()
     swap_copy = send(root_all.at[my_half], root_all.at[my_half], swap_sem, 0, other_core)
-    down_part(1, 0)
-    for copy in map_copies:
-        copy.wait_recv()
-    map_high, map_low = halves(root_map[...])
     swap_copy.wait_recv()
     root_term = dot_split(root_all[...], map_high, map_low, NN)
-    down_part(1, 1)
+    for j in range(CHUNKS):
+        down_send(down_value(2, j) - root_term[j * chunk:(j + 1) * chunk], 1, j)
+    for j in range(CHUNKS):
+        down_send(down_value(1, j), 0, j)
 
     back_copies = {}
     for j in range(CHUNKS):
-        rows = pl.ds(j * chunk, chunk)
-        down_take(0, j)
-        value = leaf[0, rows] - root_term[j * chunk:(j + 1) * chunk]
+        value = down_value(0, j)
         spot = pl.ds(pl.multiple_of(x * slice_cols + j * chunk, chunk), chunk)
         back[spot] = jnp.where(live, value, 0.0).astype(BF16)
         for k in leaf_order[:-1]:
@@ -311,16 +289,18 @@
         vmem(butterfly.shape, BF16), vmem(butterfly.shape, BF16),
         vmem((width, width), BF16), vmem((width, width), BF16),
         vmem((n_sub, slice_cols, width), F32), vmem((n_sub, slice_cols, width), F32),
-        vmem((levels + 1, slice_cols, width), F32), vmem((levels, slice_cols, width), F32),
+        vmem((levels + 1, slice_cols, width), F32), vmem((slice_cols, width), F32),
         vmem((levels, slice_cols, width), BF16), vmem((levels, slice_cols, width), BF16),
-        vmem((levels + 1, root_rows, width), F32), vmem((levels, root_rows, width), F32),
-        vmem((levels, root_rows, width), F32), vmem((width, width), F32), vmem((width, width), F32),
+        vmem((slice_cols, width), F32), vmem((slice_cols, width), F32),
+        vmem((levels, slice_cols, width), BF16), vmem((levels, slice_cols, width), BF16),
+        vmem((2, root_rows, width), F32), vmem((root_rows, width), F32), vmem((root_rows, width), F32),
+        vmem((width, width), F32),
         vmem((slice_cols, width), F32), vmem((half, width), F32), vmem((n_y, piece, width), F32),
         vmem((piece, width), F32), vmem((n_z, piece, width), F32), vmem((piece, width), F32),
         vmem((slice_cols, width), F32),
         vmem((columns, width), BF16), vmem((points, columns), F32),
         pltpu.SemaphoreType.DMA((7,)), pltpu.SemaphoreType.DMA((n_sub,)),
-        pair(CHUNKS * n_sub), pair(levels * CHUNKS), pair(levels * CHUNKS), pair(levels), pair(n_sub), pair(n_sub),
+        pair(CHUNKS * n_sub), pair(levels * CHUNKS), pair(levels * CHUNKS), pair(1), pair(n_sub),
         pair(1), pair(n_y), pair(n_z), pair(n_y), pair(1), pair(CHUNKS * n_sub),
     ]
     hbm = pl.BlockSpec(memory_space=pl.ANY)

time: 66.3 us -> 66.7 us (level)
  no operation moved by 1% of the time
where the time goes in v3:
time: 66.7 us; the launch traced here: 66.2 us
  Pallas kernels  63.7 us (96%)
  local copies, waits for them, and re-layouts  1.87 us (3%)
    pallas_call x1, Pallas kernels, local(): pl.pallas_call(functools.partial(kernel, n_y, n_z, n_sub, levels), out_sh...  63.7 us
    unnamed x1, local copies, waits for them, and re-layouts  1.87 us

profile of v3, /device:TPU:1, one launch (start us, length us, event | category | flops | bytes accessed | tf_op | source)
XLA Modules:
  0.0 66.2 jit_solution(6210371112011012197)
XLA Ops:
  0.7 63.7 %shard_map.64 = f32[256,512]{1,0:T(8,128)} custom-call(bf16[256,512]{1,0:T(8,128)(2,1)} %rhs_hbm.1, bf16[256,256]{1,0:T(8,128)(2,1)} %interp_hbm.1, s32[1]{0:T(128)S(6)} %copy.8.count_ref, f32[3,256,512]{2,1,0:T(8,128)} %butterfly_hbm.1, f32[256,256]{1,0:T(8,128)} %project_hbm.1, f32[256,256]{1,0:T(8,128)} %inverse_hbm.1), custom_call_target="tpu_custom_call" | custom-call | tf_op jit(solution)/shard_map/pallas_call | solution.py:307
  64.3 1.9 %copy.9 = f32[256,512]{1,0:T(8,128)} copy(f32[256,512]{1,0:T(8,128)} %shard_map.64) | data formatting | bytes 1048576

commit v4 on v3

--- a/solution.py
+++ b/solution.py
@@ -39,10 +39,10 @@
     rhs, interp, interp_t, butterfly, inverse,
     weight_high, weight_low, inverse_high, inverse_low,
     leaf, leaf_in, up, up_wide_in, up_out, up_in, down_wide_out, down_wide_in, down_out, down_in,
-    sweep, sweep_out, sweep_in, root_map,
+    sweep, sweep_out, sweep_in, step_map, root_map,
     root_part, root_core, root_y, root_mine, root_z, root_piece, root_all,
     back, out,
-    load_sem, out_sem, leaf_sem, up_sem, down_sem, sweep_sem, map_sem, core_sem, y_sem, z_sem, spread_sem,
+    load_sem, out_sem, leaf_sem, up_sem, down_sem, sweep_sem, step_sem, map_sem, core_sem, y_sem, z_sem, spread_sem,
     swap_sem, back_sem,
 ):
     width = interp.shape[0]
@@ -87,7 +87,7 @@
     my_rows = pl.ds(pl.multiple_of(x * root_rows, root_rows), root_rows)
     loads = []
     for source, target in (
-        (interp_hbm, interp), (rhs_hbm, rhs), (project_hbm.at[my_rows], sweep.at[1]),
+        (interp_hbm, interp), (rhs_hbm, rhs), (project_hbm.at[my_rows], sweep.at[levels]),
         (butterfly_hbm.at[2], butterfly.at[2]), (butterfly_hbm.at[0], butterfly.at[0]),
         (butterfly_hbm.at[1], butterfly.at[1]), (inverse_hbm, inverse),
     ):
@@ -128,12 +128,28 @@
     def cross(value, level, dims):
         return dot_split(value, weight_high[level, :, width:], weight_low[level, :, width:], dims)
 
+    sweep_copies = {}
+
+    def sweep_send(level):
+        sweep_out[level] = cross(sweep[level + 1], level, NN)
+        sweep_copies[level] = send(
+            sweep_out.at[level], sweep_in.at[level], sweep_sem, level, sibling(level))
+        sweep[level] = own(sweep[level + 1], level, NN)
+
+    def sweep_take(level):
+        sweep_copies[level].wait_recv()
+        sweep[level] = sweep[level] + sweep_in[level]
+        if level > 0:
+            sweep_send(level - 1)
+
+    def gather(level, target, sems):
+        target[my_rows] = sweep[level]
+        return [send(sweep.at[level], target.at[my_rows], sems, k, at_x(k)) for k in range(1, n_sub)]
+
     loads[2].wait()
     loads[3].wait()
     split_level(2)
-    sweep_out[...] = cross(sweep[1], levels - 1, NN)
-    sweep_copy = send(sweep_out, sweep_in, sweep_sem, 0, sibling(levels - 1))
-    sweep[0] = own(sweep[1], levels - 1, NN)
+    sweep_send(levels - 1)
     for position, level in ((4, 0), (5, 1)):
         loads[position].wait()
         split_level(level)
@@ -194,25 +210,31 @@
         arrived = down_in[level, rows].astype(F32) if level else down_wide_in[rows]
         return down_own[j] + arrived
 
+    def down_step(level, j):
+        down_send(down_value(level, j), level - 1, j)
+
+    def parts(step, level, part):
+        for j in range(part * CHUNKS // 2, (part + 1) * CHUNKS // 2):
+            step(level, j)
+
     for j in range(CHUNKS):
         up_start(j)
-    sweep_copy.wait_recv()
-    sweep[0] = sweep[0] + sweep_in[...]
-    root_map[my_rows] = sweep[0]
-    map_copies = [send(sweep.at[0], root_map.at[my_rows], map_sem, k, at_x(k)) for k in range(1, n_sub)]
-    for j in range(CHUNKS):
-        up_step(0, j)
-    for copy in map_copies:
-        copy.wait_recv()
-    map_high, map_low = halves(root_map[...])
+    sweep_take(2)
+    step_copies = gather(2, step_map, step_sem)
+    parts(up_step, 0, 0)
+    parts(up_step, 0, 1)
+    for copy in step_copies:
+        copy.wait_recv()
+    step_high, step_low = halves(step_map[...])
 
     my_half = pl.ds(pl.multiple_of(core * half, half), half)
     other_half = pl.ds(pl.multiple_of((1 - core) * half, half), half)
     for j in range(CHUNKS):
         rows = pl.ds(j * chunk, chunk)
         up_step(1, j)
-        root_part[rows] = dot_split(up[levels - 1, rows], map_high, map_low, NT)
+        root_part[rows] = dot_split(up[levels - 1, rows], step_high, step_low, NT)
     core_copy = send(root_part.at[other_half], root_core, core_sem, 0, other_core)
+    sweep_take(1)
 
     def piece_of(k):
         return pl.ds(pl.multiple_of(((y + k) % n_y) * piece, piece), piece)
@@ -220,14 +242,16 @@
     core_copy.wait_recv()
     root_core[...] = root_core[...] + root_part[my_half]
     y_copies = [send(root_core.at[piece_of(k)], root_y.at[k], y_sem, k, at_y(k)) for k in range(1, n_y)]
+    parts(up_step, 2, 0)
     total = root_core[piece_of(0)]
     for k, copy in enumerate(y_copies, 1):
         copy.wait_recv()
         total = total + root_y[k]
     root_mine[...] = total
     z_copies = [send(root_mine, root_z.at[k], z_sem, k, at_z(k)) for k in range(1, n_z)]
-    for j in range(CHUNKS):
-        up_step(2, j)
+    parts(up_step, 2, 1)
+    sweep_take(0)
+    map_copies = gather(0, root_map, map_sem)
     for k, copy in enumerate(z_copies, 1):
         copy.wait_recv()
         total = total + root_z[k]
@@ -238,19 +262,22 @@
     root_all[mine] = solved
     spread_copies = [
         send(root_piece, root_all.at[mine], spread_sem, k, at_y(k)) for k in range(1, n_y)]
+    parts(down_step, 2, 0)
+    parts(down_step, 2, 1)
     for copy in spread_copies:
         copy.wait_recv()
     swap_copy = send(root_all.at[my_half], root_all.at[my_half], swap_sem, 0, other_core)
+    parts(down_step, 1, 0)
+    parts(down_step, 1, 1)
+    for copy in map_copies:
+        copy.wait_recv()
+    map_high, map_low = halves(root_map[...])
     swap_copy.wait_recv()
     root_term = dot_split(root_all[...], map_high, map_low, NN)
-    for j in range(CHUNKS):
-        down_send(down_value(2, j) - root_term[j * chunk:(j + 1) * chunk], 1, j)
-    for j in range(CHUNKS):
-        down_send(down_value(1, j), 0, j)
 
     back_copies = {}
     for j in range(CHUNKS):
-        value = down_value(0, j)
+        value = down_value(0, j) - root_term[j * chunk:(j + 1) * chunk]
         spot = pl.ds(pl.multiple_of(x * slice_cols + j * chunk, chunk), chunk)
         back[spot] = jnp.where(live, value, 0.0).astype(BF16)
         for k in leaf_order[:-1]:
@@ -293,14 +320,14 @@
         vmem((levels, slice_cols, width), BF16), vmem((levels, slice_cols, width), BF16),
         vmem((slice_cols, width), F32), vmem((slice_cols, width), F32),
         vmem((levels, slice_cols, width), BF16), vmem((levels, slice_cols, width), BF16),
-        vmem((2, root_rows, width), F32), vmem((root_rows, width), F32), vmem((root_rows, width), F32),
-        vmem((width, width), F32),
+        vmem((levels + 1, root_rows, width), F32), vmem((levels, root_rows, width), F32),
+        vmem((levels, root_rows, width), F32), vmem((width, width), F32), vmem((width, width), F32),
         vmem((slice_cols, width), F32), vmem((half, width), F32), vmem((n_y, piece, width), F32),
         vmem((piece, width), F32), vmem((n_z, piece, width), F32), vmem((piece, width), F32),
         vmem((slice_cols, width), F32),
         vmem((columns, width), BF16), vmem((points, columns), F32),
         pltpu.SemaphoreType.DMA((7,)), pltpu.SemaphoreType.DMA((n_sub,)),
-        pair(CHUNKS * n_sub), pair(levels * CHUNKS), pair(levels * CHUNKS), pair(1), pair(n_sub),
+        pair(CHUNKS * n_sub), pair(levels * CHUNKS), pair(levels * CHUNKS), pair(levels), pair(n_sub), pair(n_sub),
         pair(1), pair(n_y), pair(n_z), pair(n_y), pair(1), pair(CHUNKS * n_sub),
     ]
     hbm = pl.BlockSpec(memory_space=pl.ANY)

time: 66.7 us -> 60.3 us (0.904)
  Pallas kernels: 63.7 us -> 56.9 us
    pallas_call x1, Pallas kernels: 63.7 us -> 56.9 us  [local(): pl.pallas_call(functools.partial(kernel, n_y, n_z, n_sub, levels), out_sh...]
where the time goes in v4:
time: 60.3 us; the launch traced here: 59.5 us
  Pallas kernels  56.9 us (94%)
  local copies, waits for them, and re-layouts  1.87 us (3%)
  between operations  0.66 us (1%)
    pallas_call x1, Pallas kernels, local(): pl.pallas_call(functools.partial(kernel, n_y, n_z, n_sub, levels), out_sh...  56.9 us
    unnamed x1, local copies, waits for them, and re-layouts  1.87 us

profile of v4, /device:TPU:1, one launch (start us, length us, event | category | flops | bytes accessed | tf_op | source)
XLA Modules:
  0.0 59.5 jit_solution(15727228897952792794)
XLA Ops:
  0.7 56.9 %shard_map.64 = f32[256,512]{1,0:T(8,128)} custom-call(bf16[256,512]{1,0:T(8,128)(2,1)} %rhs_hbm.1, bf16[256,256]{1,0:T(8,128)(2,1)} %interp_hbm.1, s32[1]{0:T(128)S(6)} %copy.8.count_ref, f32[3,256,512]{2,1,0:T(8,128)} %butterfly_hbm.1, f32[256,256]{1,0:T(8,128)} %project_hbm.1, f32[256,256]{1,0:T(8,128)} %inverse_hbm.1), custom_call_target="tpu_custom_call" | custom-call | tf_op jit(solution)/shard_map/pallas_call | solution.py:334
  57.6 1.9 %copy.9 = f32[256,512]{1,0:T(8,128)} copy(f32[256,512]{1,0:T(8,128)} %shard_map.64) | data formatting | bytes 1048576

commit v5 on v4

--- a/solution.py
+++ b/solution.py
@@ -34,44 +34,39 @@
 
 
 def kernel(
-    n_y, n_z, n_sub, levels,
+    n_plane, n_z, n_sub, levels,
     rhs_hbm, interp_hbm, count_ref, butterfly_hbm, project_hbm, inverse_hbm, out_hbm,
     rhs, interp, interp_t, butterfly, inverse,
     weight_high, weight_low, inverse_high, inverse_low,
     leaf, leaf_in, up, up_wide_in, up_out, up_in, down_wide_out, down_wide_in, down_out, down_in,
     sweep, sweep_out, sweep_in, step_map, root_map,
-    root_part, root_core, root_y, root_mine, root_z, root_piece, root_all,
+    root_part, root_plane, root_mine, root_z, root_piece, root_all,
     back, out,
-    load_sem, out_sem, leaf_sem, up_sem, down_sem, sweep_sem, step_sem, map_sem, core_sem, y_sem, z_sem, spread_sem,
-    swap_sem, back_sem,
+    load_sem, out_sem, leaf_sem, up_sem, down_sem, sweep_sem, step_sem, map_sem, plane_sem, z_sem, spread_sem, back_sem,
 ):
     width = interp.shape[0]
     slice_cols = leaf.shape[1]
-    half = slice_cols // 2
     chunk = slice_cols // CHUNKS
     root_rows = width // n_sub
-    piece = half // n_y
+    piece = slice_cols // n_plane
 
     box = lax.axis_index("box")
     x = lax.axis_index("sub")
-    core = box % 2
-    y = (box // 2) % n_y
-    z = box // (2 * n_y)
+    place = box % n_plane
+    z = box // n_plane
 
     def at_x(k):
         return (box, (x + k) % n_sub)
 
-    def at_y(k):
-        return (z * 2 * n_y + ((y + k) % n_y) * 2 + core, x)
+    def at_place(k):
+        return (z * n_plane + (place + k) % n_plane, x)
 
     def at_z(k):
-        return (((z + k) % n_z) * 2 * n_y + y * 2 + core, x)
+        return (((z + k) % n_z) * n_plane + place, x)
 
     def sibling(level):
         bit = 2 ** level
-        return (box + (1 - 2 * ((z // bit) % 2)) * bit * 2 * n_y, x)
-
-    other_core = (box + 1 - 2 * core, x)
+        return (box + (1 - 2 * ((z // bit) % 2)) * bit * n_plane, x)
 
     def send(source, target, sems, index, device):
         copy = pltpu.make_async_remote_copy(
@@ -96,26 +91,30 @@
         loads.append(load)
 
     barrier = pltpu.get_barrier_semaphore()
-    peers = ([at_x(k) for k in range(1, n_sub)] + [at_y(k) for k in range(1, n_y)]
-             + [at_z(k) for k in range(1, n_z)] + [other_core])
+    peers = ([at_x(k) for k in range(1, n_sub)] + [at_place(k) for k in range(1, n_plane)]
+             + [at_z(k) for k in range(1, n_z)])
     for peer in peers:
         pl.semaphore_signal(barrier, inc=1, device_id=peer, device_id_type=MESH)
 
     leaf_order = sorted(range(n_sub), key=lambda k: (k == 0, -min(k, n_sub - k)))
+    leaf_copies = {}
+
+    def leaf_send(j, k):
+        rows = pl.ds(j * chunk, chunk)
+        leaf_copies[j, k] = send(leaf.at[k, rows], leaf_in.at[k, rows], leaf_sem, j * n_sub + k, at_x(k))
+
     loads[0].wait()
     loads[1].wait()
+    pl.semaphore_wait(barrier, len(peers))
     interp_value = interp[...]
     for k in leaf_order:
         columns = pl.ds(pl.multiple_of(((x + k) % n_sub) * slice_cols, slice_cols), slice_cols)
         leaf[k] = dot(rhs[:, columns].T, interp_value, NT)
-
-    pl.semaphore_wait(barrier, len(peers))
-
-    leaf_copies = {}
-    for j in range(CHUNKS):
-        rows = pl.ds(j * chunk, chunk)
+        if k:
+            leaf_send(0, k)
+    for j in range(1, CHUNKS):
         for k in leaf_order[:-1]:
-            leaf_copies[j, k] = send(leaf.at[k, rows], leaf_in.at[k, rows], leaf_sem, j * n_sub + k, at_x(k))
+            leaf_send(j, k)
 
     def split_level(level):
         high, low = halves(butterfly[level])
@@ -227,52 +226,45 @@
         copy.wait_recv()
     step_high, step_low = halves(step_map[...])
 
-    my_half = pl.ds(pl.multiple_of(core * half, half), half)
-    other_half = pl.ds(pl.multiple_of((1 - core) * half, half), half)
     for j in range(CHUNKS):
         rows = pl.ds(j * chunk, chunk)
         up_step(1, j)
         root_part[rows] = dot_split(up[levels - 1, rows], step_high, step_low, NT)
-    core_copy = send(root_part.at[other_half], root_core, core_sem, 0, other_core)
+
+    def piece_of(k):
+        return pl.ds(pl.multiple_of(((place + k) % n_plane) * piece, piece), piece)
+
+    plane_copies = [
+        send(root_part.at[piece_of(k)], root_plane.at[k], plane_sem, k, at_place(k)) for k in range(1, n_plane)]
     sweep_take(1)
-
-    def piece_of(k):
-        return pl.ds(pl.multiple_of(((y + k) % n_y) * piece, piece), piece)
-
-    core_copy.wait_recv()
-    root_core[...] = root_core[...] + root_part[my_half]
-    y_copies = [send(root_core.at[piece_of(k)], root_y.at[k], y_sem, k, at_y(k)) for k in range(1, n_y)]
     parts(up_step, 2, 0)
-    total = root_core[piece_of(0)]
-    for k, copy in enumerate(y_copies, 1):
-        copy.wait_recv()
-        total = total + root_y[k]
+    total = root_part[piece_of(0)]
+    for k, copy in enumerate(plane_copies, 1):
+        copy.wait_recv()
+        total = total + root_plane[k]
     root_mine[...] = total
     z_copies = [send(root_mine, root_z.at[k], z_sem, k, at_z(k)) for k in range(1, n_z)]
     parts(up_step, 2, 1)
     sweep_take(0)
     map_copies = gather(0, root_map, map_sem)
+    parts(down_step, 2, 0)
     for k, copy in enumerate(z_copies, 1):
         copy.wait_recv()
         total = total + root_z[k]
     padded = jnp.concatenate([total, jnp.zeros_like(total)], axis=0)
     solved = dot_split(padded, inverse_high[...], inverse_low[...], NT)[:piece]
     root_piece[...] = solved
-    mine = pl.ds(pl.multiple_of(core * half + y * piece, piece), piece)
-    root_all[mine] = solved
+    root_all[piece_of(0)] = solved
     spread_copies = [
-        send(root_piece, root_all.at[mine], spread_sem, k, at_y(k)) for k in range(1, n_y)]
-    parts(down_step, 2, 0)
+        send(root_piece, root_all.at[piece_of(0)], spread_sem, k, at_place(k)) for k in range(1, n_plane)]
     parts(down_step, 2, 1)
-    for copy in spread_copies:
-        copy.wait_recv()
-    swap_copy = send(root_all.at[my_half], root_all.at[my_half], swap_sem, 0, other_core)
     parts(down_step, 1, 0)
     parts(down_step, 1, 1)
     for copy in map_copies:
         copy.wait_recv()
     map_high, map_low = halves(root_map[...])
-    swap_copy.wait_recv()
+    for copy in spread_copies:
+        copy.wait_recv()
     root_term = dot_split(root_all[...], map_high, map_low, NN)
 
     back_copies = {}
@@ -300,13 +292,12 @@
         copy.wait()
 
 
-def local(n_y, n_z, n_sub, rhs_points, interp, skel_count, butterfly, project, root_inverse):
+def local(n_plane, n_z, n_sub, rhs_points, interp, skel_count, butterfly, project, root_inverse):
     points, columns = rhs_points.shape
     width = interp.shape[0]
     levels = butterfly.shape[0]
     slice_cols = columns // n_sub
-    half = slice_cols // 2
-    piece = half // n_y
+    piece = slice_cols // n_plane
     root_rows = width // n_sub
     vmem = pltpu.VMEM
     pair = lambda count: pltpu.SemaphoreType.DMA((2, count))
@@ -322,17 +313,17 @@
         vmem((levels, slice_cols, width), BF16), vmem((levels, slice_cols, width), BF16),
         vmem((levels + 1, root_rows, width), F32), vmem((levels, root_rows, width), F32),
         vmem((levels, root_rows, width), F32), vmem((width, width), F32), vmem((width, width), F32),
-        vmem((slice_cols, width), F32), vmem((half, width), F32), vmem((n_y, piece, width), F32),
+        vmem((slice_cols, width), F32), vmem((n_plane, piece, width), F32),
         vmem((piece, width), F32), vmem((n_z, piece, width), F32), vmem((piece, width), F32),
         vmem((slice_cols, width), F32),
         vmem((columns, width), BF16), vmem((points, columns), F32),
         pltpu.SemaphoreType.DMA((7,)), pltpu.SemaphoreType.DMA((n_sub,)),
         pair(CHUNKS * n_sub), pair(levels * CHUNKS), pair(levels * CHUNKS), pair(levels), pair(n_sub), pair(n_sub),
-        pair(1), pair(n_y), pair(n_z), pair(n_y), pair(1), pair(CHUNKS * n_sub),
+        pair(n_plane), pair(n_z), pair(n_plane), pair(CHUNKS * n_sub),
     ]
     hbm = pl.BlockSpec(memory_space=pl.ANY)
     return pl.pallas_call(
-        functools.partial(kernel, n_y, n_z, n_sub, levels),
+        functools.partial(kernel, n_plane, n_z, n_sub, levels),
         out_shape=jax.ShapeDtypeStruct((points, columns), F32),
         in_specs=[hbm, hbm, pl.BlockSpec(memory_space=pltpu.SMEM), hbm, hbm, hbm],
         out_specs=pl.BlockSpec(memory_space=pl.ANY),
@@ -345,7 +336,6 @@
 def solution(mesh):
     n_box, n_sub = mesh.shape["box"], mesh.shape["sub"]
     n_z = 8
-    n_y = n_box // (2 * n_z)
     in_specs = (
         P(("box", "sub"), None),
         P(("box", "sub"), None),
@@ -356,5 +346,5 @@
     )
     out_specs = P(("box", "sub"), None)
     return jax.shard_map(
-        functools.partial(local, n_y, n_z, n_sub),
+        functools.partial(local, n_box // n_z, n_z, n_sub),
         mesh=mesh, in_specs=in_specs, out_specs=out_specs, check_vma=False)

time: 60.3 us -> 60.4 us (level); the launches traced: 59.5 us -> 60.3 us
  Pallas kernels: 56.9 us -> 57.7 us
    pallas_call x1, Pallas kernels: 56.9 us -> 57.7 us  [local(): pl.pallas_call(functools.partial(kernel, n_plane, n_z, n_sub, levels), ou...]
where the time goes in v5:
time: 60.4 us; the launch traced here: 60.3 us
  Pallas kernels  57.7 us (96%)
  local copies, waits for them, and re-layouts  1.87 us (3%)
  between operations  0.66 us (1%)
    pallas_call x1, Pallas kernels, local(): pl.pallas_call(functools.partial(kernel, n_plane, n_z, n_sub, levels), ou...  57.7 us
    unnamed x1, local copies, waits for them, and re-layouts  1.87 us

profile of v5, /device:TPU:1, one launch (start us, length us, event | category | flops | bytes accessed | tf_op | source)
XLA Modules:
  0.0 60.3 jit_solution(13108063313273528495)
XLA Ops:
  0.7 57.7 %shard_map.64 = f32[256,512]{1,0:T(8,128)} custom-call(bf16[256,512]{1,0:T(8,128)(2,1)} %rhs_hbm.1, bf16[256,256]{1,0:T(8,128)(2,1)} %interp_hbm.1, s32[1]{0:T(128)S(6)} %copy.8.count_ref, f32[3,256,512]{2,1,0:T(8,128)} %butterfly_hbm.1, f32[256,256]{1,0:T(8,128)} %project_hbm.1, f32[256,256]{1,0:T(8,128)} %inverse_hbm.1), custom_call_target="tpu_custom_call" | custom-call | tf_op jit(solution)/shard_map/pallas_call | solution.py:325
  58.4 1.9 %copy.9 = f32[256,512]{1,0:T(8,128)} copy(f32[256,512]{1,0:T(8,128)} %shard_map.64) | data formatting | bytes 1048576

commit v6 on v5

--- a/solution.py
+++ b/solution.py
@@ -10,7 +10,7 @@
 F32 = jnp.float32
 BF16 = jnp.bfloat16
 MESH = pl.DeviceIdType.MESH
-CHUNKS = 2
+CHUNKS = 4
 NN = (((1,), (0,)), ((), ()))
 NT = (((1,), (1,)), ((), ()))
 

time: 60.4 us -> 61.4 us (1.017)
  Pallas kernels: 57.7 us -> 58.5 us
    pallas_call x1, Pallas kernels: 57.7 us -> 58.5 us  [local(): pl.pallas_call(functools.partial(kernel, n_plane, n_z, n_sub, levels), ou...]
where the time goes in v6:
time: 61.4 us; the launch traced here: 61 us
  Pallas kernels  58.5 us (95%)
  local copies, waits for them, and re-layouts  1.87 us (3%)
  between operations  0.66 us (1%)
    pallas_call x1, Pallas kernels, local(): pl.pallas_call(functools.partial(kernel, n_plane, n_z, n_sub, levels), ou...  58.5 us
    unnamed x1, local copies, waits for them, and re-layouts  1.87 us

profile of v6, /device:TPU:1, one launch (start us, length us, event | category | flops | bytes accessed | tf_op | source)
XLA Modules:
  0.0 61.0 jit_solution(9792684693073761454)
XLA Ops:
  0.7 58.5 %shard_map.64 = f32[256,512]{1,0:T(8,128)} custom-call(bf16[256,512]{1,0:T(8,128)(2,1)} %rhs_hbm.1, bf16[256,256]{1,0:T(8,128)(2,1)} %interp_hbm.1, s32[1]{0:T(128)S(6)} %copy.8.count_ref, f32[3,256,512]{2,1,0:T(8,128)} %butterfly_hbm.1, f32[256,256]{1,0:T(8,128)} %project_hbm.1, f32[256,256]{1,0:T(8,128)} %inverse_hbm.1), custom_call_target="tpu_custom_call" | custom-call | tf_op jit(solution)/shard_map/pallas_call | solution.py:325
  59.2 1.9 %copy.9 = f32[256,512]{1,0:T(8,128)} copy(f32[256,512]{1,0:T(8,128)} %shard_map.64) | data formatting | bytes 1048576

commit v7 on v5

--- a/solution.py
+++ b/solution.py
@@ -38,11 +38,11 @@
     rhs_hbm, interp_hbm, count_ref, butterfly_hbm, project_hbm, inverse_hbm, out_hbm,
     rhs, interp, interp_t, butterfly, inverse,
     weight_high, weight_low, inverse_high, inverse_low,
-    leaf, leaf_in, up, up_wide_in, up_out, up_in, down_wide_out, down_wide_in, down_out, down_in,
+    leaf, leaf_in, relay_in, relay_out, up, up_wide_in, up_out, up_in, down_wide_out, down_wide_in, down_out, down_in,
     sweep, sweep_out, sweep_in, step_map, root_map,
     root_part, root_plane, root_mine, root_z, root_piece, root_all,
     back, out,
-    load_sem, out_sem, leaf_sem, up_sem, down_sem, sweep_sem, step_sem, map_sem, plane_sem, z_sem, spread_sem, back_sem,
+    load_sem, out_sem, leaf_sem, relay_sem, up_sem, down_sem, sweep_sem, step_sem, map_sem, plane_sem, z_sem, spread_sem, back_sem,
 ):
     width = interp.shape[0]
     slice_cols = leaf.shape[1]
@@ -96,25 +96,31 @@
     for peer in peers:
         pl.semaphore_signal(barrier, inc=1, device_id=peer, device_id_type=MESH)
 
-    leaf_order = sorted(range(n_sub), key=lambda k: (k == 0, -min(k, n_sub - k)))
+    ahead, behind, across = 1, n_sub - 1, n_sub // 2
     leaf_copies = {}
 
-    def leaf_send(j, k):
-        rows = pl.ds(j * chunk, chunk)
-        leaf_copies[j, k] = send(leaf.at[k, rows], leaf_in.at[k, rows], leaf_sem, j * n_sub + k, at_x(k))
+    def rows_of(j):
+        return pl.ds(j * chunk, chunk)
+
+    def leaf_send(j, k, source):
+        leaf_copies[j, k] = send(source, leaf_in.at[k, rows_of(j)], leaf_sem, j * n_sub + k, at_x(k))
+
+    def leaf_term(k):
+        columns = pl.ds(pl.multiple_of(((x + k) % n_sub) * slice_cols, slice_cols), slice_cols)
+        leaf[k] = dot(rhs[:, columns].T, interp_value, NT)
 
     loads[0].wait()
     loads[1].wait()
     pl.semaphore_wait(barrier, len(peers))
     interp_value = interp[...]
-    for k in leaf_order:
-        columns = pl.ds(pl.multiple_of(((x + k) % n_sub) * slice_cols, slice_cols), slice_cols)
-        leaf[k] = dot(rhs[:, columns].T, interp_value, NT)
-        if k:
-            leaf_send(0, k)
-    for j in range(1, CHUNKS):
-        for k in leaf_order[:-1]:
-            leaf_send(j, k)
+    leaf_term(across)
+    relay_copies = [
+        send(leaf.at[across, rows_of(j)], relay_in.at[j], relay_sem, j, at_x(k)) for j, k in enumerate((ahead, behind))]
+    leaf_term(behind)
+    leaf_send(0, behind, leaf.at[behind, rows_of(0)])
+    leaf_term(ahead)
+    leaf_send(1, ahead, leaf.at[ahead, rows_of(1)])
+    leaf_term(0)
 
     def split_level(level):
         high, low = halves(butterfly[level])
@@ -149,6 +155,10 @@
     loads[3].wait()
     split_level(2)
     sweep_send(levels - 1)
+    for j, k in enumerate((ahead, behind)):
+        relay_copies[j].wait_recv()
+        relay_out[j] = leaf[k, rows_of(j)] + relay_in[j]
+        leaf_send(j, k, relay_out.at[j])
     for position, level in ((4, 0), (5, 1)):
         loads[position].wait()
         split_level(level)
@@ -173,7 +183,7 @@
     def up_start(j):
         rows = pl.ds(j * chunk, chunk)
         total = leaf[0, rows]
-        for k in leaf_order[:-1][::-1]:
+        for k in ((behind, ahead), (ahead, behind))[j]:
             leaf_copies[j, k].wait_recv()
             total = total + leaf_in[k, rows]
         up[0, rows] = jnp.where(live, total, 0.0)
@@ -272,19 +282,33 @@
         value = down_value(0, j) - root_term[j * chunk:(j + 1) * chunk]
         spot = pl.ds(pl.multiple_of(x * slice_cols + j * chunk, chunk), chunk)
         back[spot] = jnp.where(live, value, 0.0).astype(BF16)
-        for k in leaf_order[:-1]:
+        for k in (ahead, behind):
             back_copies[j, k] = send(back.at[spot], back.at[spot], back_sem, j * n_sub + k, at_x(k))
 
+    def place_of(k):
+        return ((x + n_sub - k) % n_sub) * slice_cols
+
     out_copies = []
-    for k in (0, *leaf_order[:-1][::-1]):
-        columns = pl.ds(pl.multiple_of(((x + n_sub - k) % n_sub) * slice_cols, slice_cols), slice_cols)
-        if k:
-            for j in range(CHUNKS):
-                back_copies[j, k].wait_recv()
+
+    def update(k):
+        columns = pl.ds(pl.multiple_of(place_of(k), slice_cols), slice_cols)
         out[:, columns] = rhs[:, columns].astype(F32) - dot(interp_t[...], back[columns], NT)
         copy = pltpu.make_async_copy(out.at[:, columns], out_hbm.at[:, columns], out_sem.at[k])
         copy.start()
         out_copies.append(copy)
+
+    passed = []
+    update(0)
+    for j, k in enumerate((ahead, behind)):
+        back_copies[j, k].wait_recv()
+        spot = pl.ds(pl.multiple_of(place_of(k) + j * chunk, chunk), chunk)
+        passed.append(send(back.at[spot], back.at[spot], back_sem, j * n_sub + across, at_x(k)))
+    for j, k in ((1, ahead), (0, behind)):
+        back_copies[j, k].wait_recv()
+        update(k)
+    for copy in passed:
+        copy.wait_recv()
+    update(across)
 
     for copy in started:
         copy.wait_send()
@@ -307,6 +331,7 @@
         vmem(butterfly.shape, BF16), vmem(butterfly.shape, BF16),
         vmem((width, width), BF16), vmem((width, width), BF16),
         vmem((n_sub, slice_cols, width), F32), vmem((n_sub, slice_cols, width), F32),
+        vmem((CHUNKS, slice_cols // CHUNKS, width), F32), vmem((CHUNKS, slice_cols // CHUNKS, width), F32),
         vmem((levels + 1, slice_cols, width), F32), vmem((slice_cols, width), F32),
         vmem((levels, slice_cols, width), BF16), vmem((levels, slice_cols, width), BF16),
         vmem((slice_cols, width), F32), vmem((slice_cols, width), F32),
@@ -318,7 +343,7 @@
         vmem((slice_cols, width), F32),
         vmem((columns, width), BF16), vmem((points, columns), F32),
         pltpu.SemaphoreType.DMA((7,)), pltpu.SemaphoreType.DMA((n_sub,)),
-        pair(CHUNKS * n_sub), pair(levels * CHUNKS), pair(levels * CHUNKS), pair(levels), pair(n_sub), pair(n_sub),
+        pair(CHUNKS * n_sub), pair(CHUNKS), pair(levels * CHUNKS), pair(levels * CHUNKS), pair(levels), pair(n_sub), pair(n_sub),
         pair(n_plane), pair(n_z), pair(n_plane), pair(CHUNKS * n_sub),
     ]
     hbm = pl.BlockSpec(memory_space=pl.ANY)

time: 60.4 us -> 62.4 us (1.033)
  Pallas kernels: 57.7 us -> 59.2 us
    pallas_call x1, Pallas kernels: 57.7 us -> 59.2 us  [local(): pl.pallas_call(functools.partial(kernel, n_plane, n_z, n_sub, levels), ou...]
where the time goes in v7:
time: 62.4 us; the launch traced here: 61.7 us
  Pallas kernels  59.2 us (95%)
  local copies, waits for them, and re-layouts  1.87 us (3%)
  between operations  0.66 us (1%)
    pallas_call x1, Pallas kernels, local(): pl.pallas_call(functools.partial(kernel, n_plane, n_z, n_sub, levels), ou...  59.2 us
    unnamed x1, local copies, waits for them, and re-layouts  1.87 us

profile of v7, /device:TPU:1, one launch (start us, length us, event | category | flops | bytes accessed | tf_op | source)
XLA Modules:
  0.0 61.7 jit_solution(10761464000096507251)
XLA Ops:
  0.7 59.2 %shard_map.64 = f32[256,512]{1,0:T(8,128)} custom-call(bf16[256,512]{1,0:T(8,128)(2,1)} %rhs_hbm.1, bf16[256,256]{1,0:T(8,128)(2,1)} %interp_hbm.1, s32[1]{0:T(128)S(6)} %copy.8.count_ref, f32[3,256,512]{2,1,0:T(8,128)} %butterfly_hbm.1, f32[256,256]{1,0:T(8,128)} %project_hbm.1, f32[256,256]{1,0:T(8,128)} %inverse_hbm.1), custom_call_target="tpu_custom_call" | custom-call | tf_op jit(solution)/shard_map/pallas_call | solution.py:350
  59.9 1.9 %copy.9 = f32[256,512]{1,0:T(8,128)} copy(f32[256,512]{1,0:T(8,128)} %shard_map.64) | data formatting | bytes 1048576

commit v8 on v5

--- a/solution.py
+++ b/solution.py
@@ -37,7 +37,7 @@
     n_plane, n_z, n_sub, levels,
     rhs_hbm, interp_hbm, count_ref, butterfly_hbm, project_hbm, inverse_hbm, out_hbm,
     rhs, interp, interp_t, butterfly, inverse,
-    weight_high, weight_low, inverse_high, inverse_low,
+    weight_high, weight_low, turned_high, turned_low, inverse_high, inverse_low,
     leaf, leaf_in, up, up_wide_in, up_out, up_in, down_wide_out, down_wide_in, down_out, down_in,
     sweep, sweep_out, sweep_in, step_map, root_map,
     root_part, root_plane, root_mine, root_z, root_piece, root_all,
@@ -79,6 +79,12 @@
 
     started = []
 
+    barrier = pltpu.get_barrier_semaphore()
+    peers = ([at_x(k) for k in range(1, n_sub)] + [at_place(k) for k in range(1, n_plane)]
+             + [at_z(k) for k in range(1, n_z)])
+    for peer in peers:
+        pl.semaphore_signal(barrier, inc=1, device_id=peer, device_id_type=MESH)
+
     my_rows = pl.ds(pl.multiple_of(x * root_rows, root_rows), root_rows)
     loads = []
     for source, target in (
@@ -89,12 +95,6 @@
         load = pltpu.make_async_copy(source, target, load_sem.at[len(loads)])
         load.start()
         loads.append(load)
-
-    barrier = pltpu.get_barrier_semaphore()
-    peers = ([at_x(k) for k in range(1, n_sub)] + [at_place(k) for k in range(1, n_plane)]
-             + [at_z(k) for k in range(1, n_z)])
-    for peer in peers:
-        pl.semaphore_signal(barrier, inc=1, device_id=peer, device_id_type=MESH)
 
     leaf_order = sorted(range(n_sub), key=lambda k: (k == 0, -min(k, n_sub - k)))
     leaf_copies = {}
@@ -121,19 +121,29 @@
         weight_high[level] = high
         weight_low[level] = low
 
-    def own(value, level, dims):
-        return dot_split(value, weight_high[level, :, :width], weight_low[level, :, :width], dims)
-
-    def cross(value, level, dims):
-        return dot_split(value, weight_high[level, :, width:], weight_low[level, :, width:], dims)
+    def turn_level(level):
+        turned_high[level] = weight_high[level].T
+        turned_low[level] = weight_low[level].T
+
+    def own(value, level):
+        return dot_split(value, weight_high[level, :, :width], weight_low[level, :, :width], NN)
+
+    def cross(value, level):
+        return dot_split(value, weight_high[level, :, width:], weight_low[level, :, width:], NN)
+
+    def own_turned(value, level):
+        return dot_split(value, turned_high[level, :width], turned_low[level, :width], NN)
+
+    def cross_turned(value, level):
+        return dot_split(value, turned_high[level, width:], turned_low[level, width:], NN)
 
     sweep_copies = {}
 
     def sweep_send(level):
-        sweep_out[level] = cross(sweep[level + 1], level, NN)
+        sweep_out[level] = cross(sweep[level + 1], level)
         sweep_copies[level] = send(
             sweep_out.at[level], sweep_in.at[level], sweep_sem, level, sibling(level))
-        sweep[level] = own(sweep[level + 1], level, NN)
+        sweep[level] = own(sweep[level + 1], level)
 
     def sweep_take(level):
         sweep_copies[level].wait_recv()
@@ -152,8 +162,10 @@
     for position, level in ((4, 0), (5, 1)):
         loads[position].wait()
         split_level(level)
+        turn_level(level)
+    turn_level(levels - 1)
     loads[6].wait()
-    inverse_high[...], inverse_low[...] = halves(inverse[...])
+    inverse_high[...], inverse_low[...] = halves(inverse[...].T)
     interp_t[...] = interp_value.T
     live = lax.broadcasted_iota(jnp.int32, (chunk, width), 1) < count_ref[0]
 
@@ -168,7 +180,7 @@
             up_out[level, rows] = up[level, rows].astype(BF16)
             source, target = up_out.at[level, rows], up_in.at[level, rows]
         up_copies[level, j] = send(source, target, up_sem, level * CHUNKS + j, sibling(level))
-        up_own[j] = own(up[level, rows], level, NT)
+        up_own[j] = own_turned(up[level, rows], level)
 
     def up_start(j):
         rows = pl.ds(j * chunk, chunk)
@@ -183,7 +195,7 @@
         rows = pl.ds(j * chunk, chunk)
         up_copies[level, j].wait_recv()
         arrived = up_in[level, rows] if level else up_wide_in[rows]
-        up[level + 1, rows] = up_own[j] + cross(arrived, level, NT)
+        up[level + 1, rows] = up_own[j] + cross_turned(arrived, level)
         if level + 1 < levels:
             up_send(level + 1, j)
         else:
@@ -195,13 +207,13 @@
     def down_send(value, level, j):
         rows = pl.ds(j * chunk, chunk)
         if level == 0:
-            down_wide_out[rows] = cross(value, level, NN)
+            down_wide_out[rows] = cross(value, level)
             source, target = down_wide_out.at[rows], down_wide_in.at[rows]
         else:
-            down_out[level, rows] = cross(value, level, NN).astype(BF16)
+            down_out[level, rows] = cross(value, level).astype(BF16)
             source, target = down_out.at[level, rows], down_in.at[level, rows]
         down_copies[level, j] = send(source, target, down_sem, level * CHUNKS + j, sibling(level))
-        down_own[j] = own(value, level, NN)
+        down_own[j] = own(value, level)
 
     def down_value(level, j):
         rows = pl.ds(j * chunk, chunk)
@@ -224,12 +236,12 @@
     parts(up_step, 0, 1)
     for copy in step_copies:
         copy.wait_recv()
-    step_high, step_low = halves(step_map[...])
+    step_high, step_low = halves(step_map[...].T)
 
     for j in range(CHUNKS):
         rows = pl.ds(j * chunk, chunk)
         up_step(1, j)
-        root_part[rows] = dot_split(up[levels - 1, rows], step_high, step_low, NT)
+        root_part[rows] = dot_split(up[levels - 1, rows], step_high, step_low, NN)
 
     def piece_of(k):
         return pl.ds(pl.multiple_of(((place + k) % n_plane) * piece, piece), piece)
@@ -252,7 +264,7 @@
         copy.wait_recv()
         total = total + root_z[k]
     padded = jnp.concatenate([total, jnp.zeros_like(total)], axis=0)
-    solved = dot_split(padded, inverse_high[...], inverse_low[...], NT)[:piece]
+    solved = dot_split(padded, inverse_high[...], inverse_low[...], NN)[:piece]
     root_piece[...] = solved
     root_all[piece_of(0)] = solved
     spread_copies = [
@@ -305,6 +317,7 @@
         vmem((points, columns), BF16), vmem((width, points), BF16), vmem((points, width), BF16),
         vmem(butterfly.shape, F32), vmem((width, width), F32),
         vmem(butterfly.shape, BF16), vmem(butterfly.shape, BF16),
+        vmem((levels, 2 * width, width), BF16), vmem((levels, 2 * width, width), BF16),
         vmem((width, width), BF16), vmem((width, width), BF16),
         vmem((n_sub, slice_cols, width), F32), vmem((n_sub, slice_cols, width), F32),
         vmem((levels + 1, slice_cols, width), F32), vmem((slice_cols, width), F32),

time: 60.4 us -> 60.1 us (level)
  no operation moved by 1% of the time
where the time goes in v8:
time: 60.1 us; the launch traced here: 59.9 us
  Pallas kernels  57.4 us (96%)
  local copies, waits for them, and re-layouts  1.87 us (3%)
  between operations  0.66 us (1%)
    pallas_call x1, Pallas kernels, local(): pl.pallas_call(functools.partial(kernel, n_plane, n_z, n_sub, levels), ou...  57.4 us
    unnamed x1, local copies, waits for them, and re-layouts  1.87 us

profile of v8, /device:TPU:1, one launch (start us, length us, event | category | flops | bytes accessed | tf_op | source)
XLA Modules:
  0.0 59.9 jit_solution(11776606152949520761)
XLA Ops:
  0.7 57.4 %shard_map.64 = f32[256,512]{1,0:T(8,128)} custom-call(bf16[256,512]{1,0:T(8,128)(2,1)} %rhs_hbm.1, bf16[256,256]{1,0:T(8,128)(2,1)} %interp_hbm.1, s32[1]{0:T(128)S(6)} %copy.8.count_ref, f32[3,256,512]{2,1,0:T(8,128)} %butterfly_hbm.1, f32[256,256]{1,0:T(8,128)} %project_hbm.1, f32[256,256]{1,0:T(8,128)} %inverse_hbm.1), custom_call_target="tpu_custom_call" | custom-call | tf_op jit(solution)/shard_map/pallas_call | solution.py:338
  58.0 1.9 %copy.9 = f32[256,512]{1,0:T(8,128)} copy(f32[256,512]{1,0:T(8,128)} %shard_map.64) | data formatting | bytes 1048576

commit v9 on v8

--- a/solution.py
+++ b/solution.py
@@ -39,7 +39,7 @@
     rhs, interp, interp_t, butterfly, inverse,
     weight_high, weight_low, turned_high, turned_low, inverse_high, inverse_low,
     leaf, leaf_in, up, up_wide_in, up_out, up_in, down_wide_out, down_wide_in, down_out, down_in,
-    sweep, sweep_out, sweep_in, step_map, root_map,
+    sweep, sweep_wide_out, sweep_wide_in, sweep_out, sweep_in, step_map, root_map,
     root_part, root_plane, root_mine, root_z, root_piece, root_all,
     back, out,
     load_sem, out_sem, leaf_sem, up_sem, down_sem, sweep_sem, step_sem, map_sem, plane_sem, z_sem, spread_sem, back_sem,
@@ -140,14 +140,20 @@
     sweep_copies = {}
 
     def sweep_send(level):
-        sweep_out[level] = cross(sweep[level + 1], level)
-        sweep_copies[level] = send(
-            sweep_out.at[level], sweep_in.at[level], sweep_sem, level, sibling(level))
+        term = cross(sweep[level + 1], level)
+        if level == levels - 1:
+            sweep_wide_out[...] = term
+            source, target = sweep_wide_out, sweep_wide_in
+        else:
+            sweep_out[level] = term.astype(BF16)
+            source, target = sweep_out.at[level], sweep_in.at[level]
+        sweep_copies[level] = send(source, target, sweep_sem, level, sibling(level))
         sweep[level] = own(sweep[level + 1], level)
 
     def sweep_take(level):
         sweep_copies[level].wait_recv()
-        sweep[level] = sweep[level] + sweep_in[level]
+        arrived = sweep_wide_in[...] if level == levels - 1 else sweep_in[level].astype(F32)
+        sweep[level] = sweep[level] + arrived
         if level > 0:
             sweep_send(level - 1)
 
@@ -234,14 +240,13 @@
     step_copies = gather(2, step_map, step_sem)
     parts(up_step, 0, 0)
     parts(up_step, 0, 1)
+    parts(up_step, 1, 0)
+    parts(up_step, 1, 1)
+
     for copy in step_copies:
         copy.wait_recv()
     step_high, step_low = halves(step_map[...].T)
-
-    for j in range(CHUNKS):
-        rows = pl.ds(j * chunk, chunk)
-        up_step(1, j)
-        root_part[rows] = dot_split(up[levels - 1, rows], step_high, step_low, NN)
+    root_part[...] = dot_split(up[levels - 1], step_high, step_low, NN)
 
     def piece_of(k):
         return pl.ds(pl.multiple_of(((place + k) % n_plane) * piece, piece), piece)
@@ -324,8 +329,9 @@
         vmem((levels, slice_cols, width), BF16), vmem((levels, slice_cols, width), BF16),
         vmem((slice_cols, width), F32), vmem((slice_cols, width), F32),
         vmem((levels, slice_cols, width), BF16), vmem((levels, slice_cols, width), BF16),
-        vmem((levels + 1, root_rows, width), F32), vmem((levels, root_rows, width), F32),
-        vmem((levels, root_rows, width), F32), vmem((width, width), F32), vmem((width, width), F32),
+        vmem((levels + 1, root_rows, width), F32), vmem((root_rows, width), F32), vmem((root_rows, width), F32),
+        vmem((levels, root_rows, width), BF16), vmem((levels, root_rows, width), BF16),
+        vmem((width, width), F32), vmem((width, width), F32),
         vmem((slice_cols, width), F32), vmem((n_plane, piece, width), F32),
         vmem((piece, width), F32), vmem((n_z, piece, width), F32), vmem((piece, width), F32),
         vmem((slice_cols, width), F32),

time: 60.1 us -> 60.1 us (level)
  no operation moved by 1% of the time
where the time goes in v9:
time: 60.1 us; the launch traced here: 59.9 us
  Pallas kernels  57.4 us (96%)
  local copies, waits for them, and re-layouts  1.87 us (3%)
  between operations  0.66 us (1%)
    pallas_call x1, Pallas kernels, local(): pl.pallas_call(functools.partial(kernel, n_plane, n_z, n_sub, levels), ou...  57.4 us
    unnamed x1, local copies, waits for them, and re-layouts  1.87 us

profile of v9, /device:TPU:1, one launch (start us, length us, event | category | flops | bytes accessed | tf_op | source)
XLA Modules:
  0.0 59.9 jit_solution(18342710850808608502)
XLA Ops:
  0.7 57.4 %shard_map.64 = f32[256,512]{1,0:T(8,128)} custom-call(bf16[256,512]{1,0:T(8,128)(2,1)} %rhs_hbm.1, bf16[256,256]{1,0:T(8,128)(2,1)} %interp_hbm.1, s32[1]{0:T(128)S(6)} %copy.8.count_ref, f32[3,256,512]{2,1,0:T(8,128)} %butterfly_hbm.1, f32[256,256]{1,0:T(8,128)} %project_hbm.1, f32[256,256]{1,0:T(8,128)} %inverse_hbm.1), custom_call_target="tpu_custom_call" | custom-call | tf_op jit(solution)/shard_map/pallas_call | solution.py:344
  58.0 1.9 %copy.9 = f32[256,512]{1,0:T(8,128)} copy(f32[256,512]{1,0:T(8,128)} %shard_map.64) | data formatting | bytes 1048576

commit v10 on v8

--- a/solution.py
+++ b/solution.py
@@ -10,7 +10,7 @@
 F32 = jnp.float32
 BF16 = jnp.bfloat16
 MESH = pl.DeviceIdType.MESH
-CHUNKS = 2
+CHUNKS = 4
 NN = (((1,), (0,)), ((), ()))
 NT = (((1,), (1,)), ((), ()))
 
@@ -38,7 +38,7 @@
     rhs_hbm, interp_hbm, count_ref, butterfly_hbm, project_hbm, inverse_hbm, out_hbm,
     rhs, interp, interp_t, butterfly, inverse,
     weight_high, weight_low, turned_high, turned_low, inverse_high, inverse_low,
-    leaf, leaf_in, up, up_wide_in, up_out, up_in, down_wide_out, down_wide_in, down_out, down_in,
+    leaf, leaf_in, up, up_wide_in, up_out, up_in, down_wide_out, down_wide_in, down_out, down_in, down,
     sweep, sweep_out, sweep_in, step_map, root_map,
     root_part, root_plane, root_mine, root_z, root_piece, root_all,
     back, out,
@@ -170,20 +170,21 @@
     live = lax.broadcasted_iota(jnp.int32, (chunk, width), 1) < count_ref[0]
 
     up_copies = {}
-    up_own = {}
+
+    def rows_of(j):
+        return pl.ds(j * chunk, chunk)
 
     def up_send(level, j):
-        rows = pl.ds(j * chunk, chunk)
+        rows = rows_of(j)
         if level == 0:
             source, target = up.at[0, rows], up_wide_in.at[rows]
         else:
             up_out[level, rows] = up[level, rows].astype(BF16)
             source, target = up_out.at[level, rows], up_in.at[level, rows]
         up_copies[level, j] = send(source, target, up_sem, level * CHUNKS + j, sibling(level))
-        up_own[j] = own_turned(up[level, rows], level)
 
     def up_start(j):
-        rows = pl.ds(j * chunk, chunk)
+        rows = rows_of(j)
         total = leaf[0, rows]
         for k in leaf_order[:-1][::-1]:
             leaf_copies[j, k].wait_recv()
@@ -192,20 +193,22 @@
         up_send(0, j)
 
     def up_step(level, j):
-        rows = pl.ds(j * chunk, chunk)
+        rows = rows_of(j)
         up_copies[level, j].wait_recv()
         arrived = up_in[level, rows] if level else up_wide_in[rows]
-        up[level + 1, rows] = up_own[j] + cross_turned(arrived, level)
+        up[level + 1, rows] = up[level + 1, rows] + cross_turned(arrived, level)
         if level + 1 < levels:
             up_send(level + 1, j)
         else:
             down_send(up[levels, rows], level, j)
 
+    def up_own(level):
+        up[level + 1] = own_turned(up[level], level)
+
     down_copies = {}
-    down_own = {}
 
     def down_send(value, level, j):
-        rows = pl.ds(j * chunk, chunk)
+        rows = rows_of(j)
         if level == 0:
             down_wide_out[rows] = cross(value, level)
             source, target = down_wide_out.at[rows], down_wide_in.at[rows]
@@ -213,53 +216,54 @@
             down_out[level, rows] = cross(value, level).astype(BF16)
             source, target = down_out.at[level, rows], down_in.at[level, rows]
         down_copies[level, j] = send(source, target, down_sem, level * CHUNKS + j, sibling(level))
-        down_own[j] = own(value, level)
 
     def down_value(level, j):
-        rows = pl.ds(j * chunk, chunk)
+        rows = rows_of(j)
         down_copies[level, j].wait_recv()
         arrived = down_in[level, rows].astype(F32) if level else down_wide_in[rows]
-        return down_own[j] + arrived
+        return down[level, rows] + arrived
 
     def down_step(level, j):
-        down_send(down_value(level, j), level - 1, j)
-
-    def parts(step, level, part):
-        for j in range(part * CHUNKS // 2, (part + 1) * CHUNKS // 2):
+        value = down_value(level, j)
+        down[level, rows_of(j)] = value
+        down_send(value, level - 1, j)
+
+    def every(step, level, part=range(CHUNKS)):
+        for j in part:
             step(level, j)
 
     for j in range(CHUNKS):
         up_start(j)
+    up_own(0)
     sweep_take(2)
     step_copies = gather(2, step_map, step_sem)
-    parts(up_step, 0, 0)
-    parts(up_step, 0, 1)
+    every(up_step, 0)
+    up_own(1)
+    every(up_step, 1)
+
     for copy in step_copies:
         copy.wait_recv()
     step_high, step_low = halves(step_map[...].T)
-
-    for j in range(CHUNKS):
-        rows = pl.ds(j * chunk, chunk)
-        up_step(1, j)
-        root_part[rows] = dot_split(up[levels - 1, rows], step_high, step_low, NN)
+    root_part[...] = dot_split(up[levels - 1], step_high, step_low, NN)
 
     def piece_of(k):
         return pl.ds(pl.multiple_of(((place + k) % n_plane) * piece, piece), piece)
 
     plane_copies = [
         send(root_part.at[piece_of(k)], root_plane.at[k], plane_sem, k, at_place(k)) for k in range(1, n_plane)]
+    up_own(2)
     sweep_take(1)
-    parts(up_step, 2, 0)
+    every(up_step, 2)
     total = root_part[piece_of(0)]
     for k, copy in enumerate(plane_copies, 1):
         copy.wait_recv()
         total = total + root_plane[k]
     root_mine[...] = total
     z_copies = [send(root_mine, root_z.at[k], z_sem, k, at_z(k)) for k in range(1, n_z)]
-    parts(up_step, 2, 1)
+    down[2] = own(up[levels], 2)
     sweep_take(0)
     map_copies = gather(0, root_map, map_sem)
-    parts(down_step, 2, 0)
+    every(down_step, 2, range(CHUNKS // 2))
     for k, copy in enumerate(z_copies, 1):
         copy.wait_recv()
         total = total + root_z[k]
@@ -269,9 +273,10 @@
     root_all[piece_of(0)] = solved
     spread_copies = [
         send(root_piece, root_all.at[piece_of(0)], spread_sem, k, at_place(k)) for k in range(1, n_plane)]
-    parts(down_step, 2, 1)
-    parts(down_step, 1, 0)
-    parts(down_step, 1, 1)
+    every(down_step, 2, range(CHUNKS // 2, CHUNKS))
+    down[1] = own(down[2], 1)
+    every(down_step, 1)
+    down[0] = own(down[1], 0)
     for copy in map_copies:
         copy.wait_recv()
     map_high, map_low = halves(root_map[...])
@@ -324,6 +329,7 @@
         vmem((levels, slice_cols, width), BF16), vmem((levels, slice_cols, width), BF16),
         vmem((slice_cols, width), F32), vmem((slice_cols, width), F32),
         vmem((levels, slice_cols, width), BF16), vmem((levels, slice_cols, width), BF16),
+        vmem((levels, slice_cols, width), F32),
         vmem((levels + 1, root_rows, width), F32), vmem((levels, root_rows, width), F32),
         vmem((levels, root_rows, width), F32), vmem((width, width), F32), vmem((width, width), F32),
         vmem((slice_cols, width), F32), vmem((n_plane, piece, width), F32),

time: 60.1 us -> 60.4 us (level); the launches traced: 59.9 us -> 59.3 us
  no operation moved by 1% of the time
where the time goes in v10:
time: 60.4 us; the launch traced here: 59.3 us
  Pallas kernels  56.8 us (94%)
  local copies, waits for them, and re-layouts  1.87 us (3%)
  between operations  0.66 us (1%)
    pallas_call x1, Pallas kernels, local(): pl.pallas_call(functools.partial(kernel, n_plane, n_z, n_sub, levels), ou...  56.8 us
    unnamed x1, local copies, waits for them, and re-layouts  1.87 us

profile of v10, /device:TPU:1, one launch (start us, length us, event | category | flops | bytes accessed | tf_op | source)
XLA Modules:
  0.0 59.3 jit_solution(3305423359644565422)
XLA Ops:
  0.7 56.8 %shard_map.64 = f32[256,512]{1,0:T(8,128)} custom-call(bf16[256,512]{1,0:T(8,128)(2,1)} %rhs_hbm.1, bf16[256,256]{1,0:T(8,128)(2,1)} %interp_hbm.1, s32[1]{0:T(128)S(6)} %copy.8.count_ref, f32[3,256,512]{2,1,0:T(8,128)} %butterfly_hbm.1, f32[256,256]{1,0:T(8,128)} %project_hbm.1, f32[256,256]{1,0:T(8,128)} %inverse_hbm.1), custom_call_target="tpu_custom_call" | custom-call | tf_op jit(solution)/shard_map/pallas_call | solution.py:344
  57.5 1.9 %copy.9 = f32[256,512]{1,0:T(8,128)} copy(f32[256,512]{1,0:T(8,128)} %shard_map.64) | data formatting | bytes 1048576

commit v11 on v10

--- a/solution.py
+++ b/solution.py
@@ -10,7 +10,7 @@
 F32 = jnp.float32
 BF16 = jnp.bfloat16
 MESH = pl.DeviceIdType.MESH
-CHUNKS = 4
+CHUNKS = 2
 NN = (((1,), (0,)), ((), ()))
 NT = (((1,), (1,)), ((), ()))
 
@@ -37,10 +37,10 @@
     n_plane, n_z, n_sub, levels,
     rhs_hbm, interp_hbm, count_ref, butterfly_hbm, project_hbm, inverse_hbm, out_hbm,
     rhs, interp, interp_t, butterfly, inverse,
-    weight_high, weight_low, turned_high, turned_low, inverse_high, inverse_low,
+    weight_high, weight_low, turned_high, turned_low, inverse_turned,
     leaf, leaf_in, up, up_wide_in, up_out, up_in, down_wide_out, down_wide_in, down_out, down_in, down,
     sweep, sweep_out, sweep_in, step_map, root_map,
-    root_part, root_plane, root_mine, root_z, root_piece, root_all,
+    root_part, root_out, root_plane, root_mine, root_z, root_piece, root_all,
     back, out,
     load_sem, out_sem, leaf_sem, up_sem, down_sem, sweep_sem, step_sem, map_sem, plane_sem, z_sem, spread_sem, back_sem,
 ):
@@ -48,7 +48,7 @@
     slice_cols = leaf.shape[1]
     chunk = slice_cols // CHUNKS
     root_rows = width // n_sub
-    piece = slice_cols // n_plane
+    piece = (2 * slice_cols // n_plane, width // 2)
 
     box = lax.axis_index("box")
     x = lax.axis_index("sub")
@@ -165,7 +165,7 @@
         turn_level(level)
     turn_level(levels - 1)
     loads[6].wait()
-    inverse_high[...], inverse_low[...] = halves(inverse[...].T)
+    inverse_turned[...] = inverse[...].T
     interp_t[...] = interp_value.T
     live = lax.broadcasted_iota(jnp.int32, (chunk, width), 1) < count_ref[0]
 
@@ -209,18 +209,19 @@
 
     def down_send(value, level, j):
         rows = rows_of(j)
-        if level == 0:
-            down_wide_out[rows] = cross(value, level)
-            source, target = down_wide_out.at[rows], down_wide_in.at[rows]
+        term = cross(value, level)
+        if level == levels - 1:
+            down_out[rows] = term.astype(BF16)
+            source, target = down_out.at[rows], down_in.at[rows]
         else:
-            down_out[level, rows] = cross(value, level).astype(BF16)
-            source, target = down_out.at[level, rows], down_in.at[level, rows]
+            down_wide_out[level, rows] = term
+            source, target = down_wide_out.at[level, rows], down_wide_in.at[level, rows]
         down_copies[level, j] = send(source, target, down_sem, level * CHUNKS + j, sibling(level))
 
     def down_value(level, j):
         rows = rows_of(j)
         down_copies[level, j].wait_recv()
-        arrived = down_in[level, rows].astype(F32) if level else down_wide_in[rows]
+        arrived = down_in[rows].astype(F32) if level == levels - 1 else down_wide_in[level, rows]
         return down[level, rows] + arrived
 
     def down_step(level, j):
@@ -239,47 +240,49 @@
     step_copies = gather(2, step_map, step_sem)
     every(up_step, 0)
     up_own(1)
-    every(up_step, 1)
-
+    every(up_step, 1, range(CHUNKS // 2))
     for copy in step_copies:
         copy.wait_recv()
     step_high, step_low = halves(step_map[...].T)
+    every(up_step, 1, range(CHUNKS // 2, CHUNKS))
+
     root_part[...] = dot_split(up[levels - 1], step_high, step_low, NN)
+    root_out[...] = root_part[...].astype(BF16)
 
     def piece_of(k):
-        return pl.ds(pl.multiple_of(((place + k) % n_plane) * piece, piece), piece)
+        index = (place + k) % n_plane
+        rows = pl.ds(pl.multiple_of(index // 2 * piece[0], piece[0]), piece[0])
+        return rows, pl.ds(pl.multiple_of(index % 2 * piece[1], piece[1]), piece[1])
 
     plane_copies = [
-        send(root_part.at[piece_of(k)], root_plane.at[k], plane_sem, k, at_place(k)) for k in range(1, n_plane)]
+        send(root_out.at[piece_of(k)], root_plane.at[k], plane_sem, k, at_place(k)) for k in range(1, n_plane)]
     up_own(2)
     sweep_take(1)
-    every(up_step, 2)
     total = root_part[piece_of(0)]
     for k, copy in enumerate(plane_copies, 1):
         copy.wait_recv()
-        total = total + root_plane[k]
-    root_mine[...] = total
+        total = total + root_plane[k].astype(F32)
+    root_mine[...] = total.astype(BF16)
     z_copies = [send(root_mine, root_z.at[k], z_sem, k, at_z(k)) for k in range(1, n_z)]
+    every(up_step, 2)
     down[2] = own(up[levels], 2)
     sweep_take(0)
     map_copies = gather(0, root_map, map_sem)
-    every(down_step, 2, range(CHUNKS // 2))
     for k, copy in enumerate(z_copies, 1):
         copy.wait_recv()
-        total = total + root_z[k]
-    padded = jnp.concatenate([total, jnp.zeros_like(total)], axis=0)
-    solved = dot_split(padded, inverse_high[...], inverse_low[...], NN)[:piece]
-    root_piece[...] = solved
-    root_all[piece_of(0)] = solved
+        total = total + root_z[k].astype(F32)
+    root_piece[...] = total.astype(BF16)
+    root_all[piece_of(0)] = total.astype(BF16)
     spread_copies = [
         send(root_piece, root_all.at[piece_of(0)], spread_sem, k, at_place(k)) for k in range(1, n_plane)]
-    every(down_step, 2, range(CHUNKS // 2, CHUNKS))
+    every(down_step, 2)
     down[1] = own(down[2], 1)
+    for copy in map_copies:
+        copy.wait_recv()
+    map_high, map_low = halves(root_map[...])
+    map_high, map_low = halves(dot_split(inverse_turned[...], map_high, map_low, NN))
     every(down_step, 1)
     down[0] = own(down[1], 0)
-    for copy in map_copies:
-        copy.wait_recv()
-    map_high, map_low = halves(root_map[...])
     for copy in spread_copies:
         copy.wait_recv()
     root_term = dot_split(root_all[...], map_high, map_low, NN)
@@ -314,7 +317,7 @@
     width = interp.shape[0]
     levels = butterfly.shape[0]
     slice_cols = columns // n_sub
-    piece = slice_cols // n_plane
+    piece = (2 * slice_cols // n_plane, width // 2)
     root_rows = width // n_sub
     vmem = pltpu.VMEM
     pair = lambda count: pltpu.SemaphoreType.DMA((2, count))
@@ -323,18 +326,17 @@
         vmem(butterfly.shape, F32), vmem((width, width), F32),
         vmem(butterfly.shape, BF16), vmem(butterfly.shape, BF16),
         vmem((levels, 2 * width, width), BF16), vmem((levels, 2 * width, width), BF16),
-        vmem((width, width), BF16), vmem((width, width), BF16),
+        vmem((width, width), F32),
         vmem((n_sub, slice_cols, width), F32), vmem((n_sub, slice_cols, width), F32),
         vmem((levels + 1, slice_cols, width), F32), vmem((slice_cols, width), F32),
         vmem((levels, slice_cols, width), BF16), vmem((levels, slice_cols, width), BF16),
-        vmem((slice_cols, width), F32), vmem((slice_cols, width), F32),
-        vmem((levels, slice_cols, width), BF16), vmem((levels, slice_cols, width), BF16),
+        vmem((levels - 1, slice_cols, width), F32), vmem((levels - 1, slice_cols, width), F32),
+        vmem((slice_cols, width), BF16), vmem((slice_cols, width), BF16),
         vmem((levels, slice_cols, width), F32),
         vmem((levels + 1, root_rows, width), F32), vmem((levels, root_rows, width), F32),
         vmem((levels, root_rows, width), F32), vmem((width, width), F32), vmem((width, width), F32),
-        vmem((slice_cols, width), F32), vmem((n_plane, piece, width), F32),
-        vmem((piece, width), F32), vmem((n_z, piece, width), F32), vmem((piece, width), F32),
-        vmem((slice_cols, width), F32),
+        vmem((slice_cols, width), F32), vmem((slice_cols, width), BF16), vmem((n_plane, *piece), BF16),
+        vmem(piece, BF16), vmem((n_z, *piece), BF16), vmem(piece, BF16), vmem((slice_cols, width), BF16),
         vmem((columns, width), BF16), vmem((points, columns), F32),
         pltpu.SemaphoreType.DMA((7,)), pltpu.SemaphoreType.DMA((n_sub,)),
         pair(CHUNKS * n_sub), pair(levels * CHUNKS), pair(levels * CHUNKS), pair(levels), pair(n_sub), pair(n_sub),

time: 60.4 us -> 60.3 us (level); the launches traced: 59.3 us -> 60.1 us
  Pallas kernels: 56.8 us -> 57.6 us
    pallas_call x1, Pallas kernels: 56.8 us -> 57.6 us  [local(): pl.pallas_call(functools.partial(kernel, n_plane, n_z, n_sub, levels), ou...]
where the time goes in v11:
time: 60.3 us; the launch traced here: 60.1 us
  Pallas kernels  57.6 us (96%)
  local copies, waits for them, and re-layouts  1.87 us (3%)
  between operations  0.66 us (1%)
    pallas_call x1, Pallas kernels, local(): pl.pallas_call(functools.partial(kernel, n_plane, n_z, n_sub, levels), ou...  57.6 us
    unnamed x1, local copies, waits for them, and re-layouts  1.87 us

profile of v11, /device:TPU:1, one launch (start us, length us, event | category | flops | bytes accessed | tf_op | source)
XLA Modules:
  0.0 60.1 jit_solution(14693361511567582675)
XLA Ops:
  0.7 57.6 %shard_map.64 = f32[256,512]{1,0:T(8,128)} custom-call(bf16[256,512]{1,0:T(8,128)(2,1)} %rhs_hbm.1, bf16[256,256]{1,0:T(8,128)(2,1)} %interp_hbm.1, s32[1]{0:T(128)S(6)} %copy.8.count_ref, f32[3,256,512]{2,1,0:T(8,128)} %butterfly_hbm.1, f32[256,256]{1,0:T(8,128)} %project_hbm.1, f32[256,256]{1,0:T(8,128)} %inverse_hbm.1), custom_call_target="tpu_custom_call" | custom-call | tf_op jit(solution)/shard_map/pallas_call | solution.py:346
  58.3 1.9 %copy.9 = f32[256,512]{1,0:T(8,128)} copy(f32[256,512]{1,0:T(8,128)} %shard_map.64) | data formatting | bytes 1048576

commit v12 on v10

--- a/solution.py
+++ b/solution.py
@@ -10,7 +10,7 @@
 F32 = jnp.float32
 BF16 = jnp.bfloat16
 MESH = pl.DeviceIdType.MESH
-CHUNKS = 4
+CHUNKS = 2
 NN = (((1,), (0,)), ((), ()))
 NT = (((1,), (1,)), ((), ()))
 
@@ -340,6 +340,7 @@
         pair(CHUNKS * n_sub), pair(levels * CHUNKS), pair(levels * CHUNKS), pair(levels), pair(n_sub), pair(n_sub),
         pair(n_plane), pair(n_z), pair(n_plane), pair(CHUNKS * n_sub),
     ]
+    in_hbm = lambda array: pltpu.with_memory_space_constraint(array, pltpu.HBM)
     hbm = pl.BlockSpec(memory_space=pl.ANY)
     return pl.pallas_call(
         functools.partial(kernel, n_plane, n_z, n_sub, levels),
@@ -348,8 +349,8 @@
         out_specs=pl.BlockSpec(memory_space=pl.ANY),
         scratch_shapes=scratch,
         compiler_params=pltpu.CompilerParams(
-            collective_id=0, has_side_effects=True, vmem_limit_bytes=62 * 2**20),
-    )(rhs_points, interp, skel_count, butterfly, project, root_inverse)
+            collective_id=0, has_side_effects=True, vmem_limit_bytes=40 * 2**20),
+    )(in_hbm(rhs_points), in_hbm(interp), skel_count, in_hbm(butterfly), in_hbm(project), in_hbm(root_inverse))
 
 
 def solution(mesh):

time: 60.4 us -> 58.8 us (0.974); the launches traced: 59.3 us -> 58.6 us
  local copies, waits for them, and re-layouts: 1.87 us -> 0.8 us
    unnamed x1, local copies, waits for them, and re-layouts: 1.87 us -> 0.8 us
where the time goes in v12:
time: 58.8 us; the launch traced here: 58.6 us
  Pallas kernels  57.2 us (97%)
  local copies, waits for them, and re-layouts  0.8 us (1%)
  between operations  0.66 us (1%)
    pallas_call x1, Pallas kernels, local(): pl.pallas_call(functools.partial(kernel, n_plane, n_z, n_sub, levels), ou...  57.2 us

profile of v12, /device:TPU:1, one launch (start us, length us, event | category | flops | bytes accessed | tf_op | source)
XLA Modules:
  0.0 58.6 jit_solution(12609086240439006871)
XLA Ops:
  0.7 57.2 %shard_map.64 = f32[256,512]{1,0:T(8,128)S(1)} custom-call(bf16[256,512]{1,0:T(8,128)(2,1)} %rhs_hbm.1, bf16[256,256]{1,0:T(8,128)(2,1)} %interp_hbm.1, s32[1]{0:T(128)S(6)} %copy.8.count_ref, f32[3,256,512]{2,1,0:T(8,128)} %butterfly_hbm.1, f32[256,256]{1,0:T(8,128)} %project_hbm.1, f32[256,256]{1,0:T(8,128)} %inverse_hbm.1), custom_call_target="tpu_custom_call" | custom-call | tf_op jit(solution)/shard_map/pallas_call | solution.py:345
  57.9 0.8 %copy.9 = f32[256,512]{1,0:T(8,128)} copy(f32[256,512]{1,0:T(8,128)S(1)} %shard_map.64) | data formatting | bytes 1048576

commit v13 on v12

--- a/solution.py
+++ b/solution.py
@@ -35,14 +35,14 @@
 
 def kernel(
     n_plane, n_z, n_sub, levels,
-    rhs_hbm, interp_hbm, count_ref, butterfly_hbm, project_hbm, inverse_hbm, out_hbm,
+    rhs_hbm, interp_hbm, count_ref, butterfly_hbm, project_hbm, inverse_hbm, out,
     rhs, interp, interp_t, butterfly, inverse,
     weight_high, weight_low, turned_high, turned_low, inverse_high, inverse_low,
-    leaf, leaf_in, up, up_wide_in, up_out, up_in, down_wide_out, down_wide_in, down_out, down_in, down,
+    leaf, leaf_in, far_out, far_in, up, up_wide_in, up_out, up_in, down_wide_out, down_wide_in, down_out, down_in, down,
     sweep, sweep_out, sweep_in, step_map, root_map,
     root_part, root_plane, root_mine, root_z, root_piece, root_all,
-    back, out,
-    load_sem, out_sem, leaf_sem, up_sem, down_sem, sweep_sem, step_sem, map_sem, plane_sem, z_sem, spread_sem, back_sem,
+    back,
+    load_sem, leaf_sem, up_sem, down_sem, sweep_sem, step_sem, map_sem, plane_sem, z_sem, spread_sem, back_sem,
 ):
     width = interp.shape[0]
     slice_cols = leaf.shape[1]
@@ -99,9 +99,15 @@
     leaf_order = sorted(range(n_sub), key=lambda k: (k == 0, -min(k, n_sub - k)))
     leaf_copies = {}
 
+    across = n_sub // 2
+
     def leaf_send(j, k):
         rows = pl.ds(j * chunk, chunk)
-        leaf_copies[j, k] = send(leaf.at[k, rows], leaf_in.at[k, rows], leaf_sem, j * n_sub + k, at_x(k))
+        if k == across:
+            source, target = far_out.at[rows], far_in.at[rows]
+        else:
+            source, target = leaf.at[k, rows], leaf_in.at[k, rows]
+        leaf_copies[j, k] = send(source, target, leaf_sem, j * n_sub + k, at_x(k))
 
     loads[0].wait()
     loads[1].wait()
@@ -109,7 +115,11 @@
     interp_value = interp[...]
     for k in leaf_order:
         columns = pl.ds(pl.multiple_of(((x + k) % n_sub) * slice_cols, slice_cols), slice_cols)
-        leaf[k] = dot(rhs[:, columns].T, interp_value, NT)
+        term = dot(rhs[:, columns].T, interp_value, NT)
+        if k == across:
+            far_out[...] = term.astype(BF16)
+        else:
+            leaf[k] = term
         if k:
             leaf_send(0, k)
     for j in range(1, CHUNKS):
@@ -188,7 +198,7 @@
         total = leaf[0, rows]
         for k in leaf_order[:-1][::-1]:
             leaf_copies[j, k].wait_recv()
-            total = total + leaf_in[k, rows]
+            total = total + (far_in[rows].astype(F32) if k == across else leaf_in[k, rows])
         up[0, rows] = jnp.where(live, total, 0.0)
         up_send(0, j)
 
@@ -292,21 +302,15 @@
         for k in leaf_order[:-1]:
             back_copies[j, k] = send(back.at[spot], back.at[spot], back_sem, j * n_sub + k, at_x(k))
 
-    out_copies = []
     for k in (0, *leaf_order[:-1][::-1]):
         columns = pl.ds(pl.multiple_of(((x + n_sub - k) % n_sub) * slice_cols, slice_cols), slice_cols)
         if k:
             for j in range(CHUNKS):
                 back_copies[j, k].wait_recv()
         out[:, columns] = rhs[:, columns].astype(F32) - dot(interp_t[...], back[columns], NT)
-        copy = pltpu.make_async_copy(out.at[:, columns], out_hbm.at[:, columns], out_sem.at[k])
-        copy.start()
-        out_copies.append(copy)
 
     for copy in started:
         copy.wait_send()
-    for copy in out_copies:
-        copy.wait()
 
 
 def local(n_plane, n_z, n_sub, rhs_points, interp, skel_count, butterfly, project, root_inverse):
@@ -325,6 +329,7 @@
         vmem((levels, 2 * width, width), BF16), vmem((levels, 2 * width, width), BF16),
         vmem((width, width), BF16), vmem((width, width), BF16),
         vmem((n_sub, slice_cols, width), F32), vmem((n_sub, slice_cols, width), F32),
+        vmem((slice_cols, width), BF16), vmem((slice_cols, width), BF16),
         vmem((levels + 1, slice_cols, width), F32), vmem((slice_cols, width), F32),
         vmem((levels, slice_cols, width), BF16), vmem((levels, slice_cols, width), BF16),
         vmem((slice_cols, width), F32), vmem((slice_cols, width), F32),
@@ -335,8 +340,8 @@
         vmem((slice_cols, width), F32), vmem((n_plane, piece, width), F32),
         vmem((piece, width), F32), vmem((n_z, piece, width), F32), vmem((piece, width), F32),
         vmem((slice_cols, width), F32),
-        vmem((columns, width), BF16), vmem((points, columns), F32),
-        pltpu.SemaphoreType.DMA((7,)), pltpu.SemaphoreType.DMA((n_sub,)),
+        vmem((columns, width), BF16),
+        pltpu.SemaphoreType.DMA((7,)),
         pair(CHUNKS * n_sub), pair(levels * CHUNKS), pair(levels * CHUNKS), pair(levels), pair(n_sub), pair(n_sub),
         pair(n_plane), pair(n_z), pair(n_plane), pair(CHUNKS * n_sub),
     ]
@@ -344,9 +349,9 @@
     hbm = pl.BlockSpec(memory_space=pl.ANY)
     return pl.pallas_call(
         functools.partial(kernel, n_plane, n_z, n_sub, levels),
-        out_shape=jax.ShapeDtypeStruct((points, columns), F32),
+        out_shape=pltpu.VMEM((points, columns), F32),
         in_specs=[hbm, hbm, pl.BlockSpec(memory_space=pltpu.SMEM), hbm, hbm, hbm],
-        out_specs=pl.BlockSpec(memory_space=pl.ANY),
+        out_specs=pl.BlockSpec(memory_space=pltpu.VMEM),
         scratch_shapes=scratch,
         compiler_params=pltpu.CompilerParams(
             collective_id=0, has_side_effects=True, vmem_limit_bytes=40 * 2**20),

time: 58.8 us -> 56.9 us (0.968)
  Pallas kernels: 57.2 us -> 55.1 us
    pallas_call x1, Pallas kernels: 57.2 us -> 55.1 us  [local(): pl.pallas_call(functools.partial(kernel, n_plane, n_z, n_sub, levels), ou...]
where the time goes in v13:
time: 56.9 us; the launch traced here: 56.6 us
  Pallas kernels  55.1 us (97%)
  local copies, waits for them, and re-layouts  0.8 us (1%)
  between operations  0.66 us (1%)
    pallas_call x1, Pallas kernels, local(): pl.pallas_call(functools.partial(kernel, n_plane, n_z, n_sub, levels), ou...  55.1 us

profile of v13, /device:TPU:1, one launch (start us, length us, event | category | flops | bytes accessed | tf_op | source)
XLA Modules:
  0.0 56.6 jit_solution(9208582066275037424)
XLA Ops:
  0.7 55.1 %shard_map.64 = f32[256,512]{1,0:T(8,128)S(1)} custom-call(bf16[256,512]{1,0:T(8,128)(2,1)} %rhs_hbm.1, bf16[256,256]{1,0:T(8,128)(2,1)} %interp_hbm.1, s32[1]{0:T(128)S(6)} %copy.9.count_ref, f32[3,256,512]{2,1,0:T(8,128)} %butterfly_hbm.1, f32[256,256]{1,0:T(8,128)} %project_hbm.1, f32[256,256]{1,0:T(8,128)} %inverse_hbm.1), custom_call_target="tpu_custom_call" | custom-call | tf_op jit(solution)/shard_map/pallas_call | solution.py:350
  55.8 0.8 %copy.8 = f32[256,512]{1,0:T(8,128)} copy(f32[256,512]{1,0:T(8,128)S(1)} %shard_map.64) | data formatting | bytes 1048576

commit v14 on v13

--- a/solution.py
+++ b/solution.py
@@ -79,22 +79,25 @@
 
     started = []
 
+    my_rows = pl.ds(pl.multiple_of(x * root_rows, root_rows), root_rows)
+    loads = []
+
+    def load(source, target):
+        copy = pltpu.make_async_copy(source, target, load_sem.at[len(loads)])
+        copy.start()
+        loads.append(copy)
+
+    load(interp_hbm, interp)
+    load(rhs_hbm, rhs)
     barrier = pltpu.get_barrier_semaphore()
     peers = ([at_x(k) for k in range(1, n_sub)] + [at_place(k) for k in range(1, n_plane)]
              + [at_z(k) for k in range(1, n_z)])
     for peer in peers:
         pl.semaphore_signal(barrier, inc=1, device_id=peer, device_id_type=MESH)
-
-    my_rows = pl.ds(pl.multiple_of(x * root_rows, root_rows), root_rows)
-    loads = []
-    for source, target in (
-        (interp_hbm, interp), (rhs_hbm, rhs), (project_hbm.at[my_rows], sweep.at[levels]),
-        (butterfly_hbm.at[2], butterfly.at[2]), (butterfly_hbm.at[0], butterfly.at[0]),
-        (butterfly_hbm.at[1], butterfly.at[1]), (inverse_hbm, inverse),
-    ):
-        load = pltpu.make_async_copy(source, target, load_sem.at[len(loads)])
-        load.start()
-        loads.append(load)
+    load(project_hbm.at[my_rows], sweep.at[levels])
+    for level in (2, 0, 1):
+        load(butterfly_hbm.at[level], butterfly.at[level])
+    load(inverse_hbm, inverse)
 
     leaf_order = sorted(range(n_sub), key=lambda k: (k == 0, -min(k, n_sub - k)))
     leaf_copies = {}
@@ -111,7 +114,6 @@
 
     loads[0].wait()
     loads[1].wait()
-    pl.semaphore_wait(barrier, len(peers))
     interp_value = interp[...]
     for k in leaf_order:
         columns = pl.ds(pl.multiple_of(((x + k) % n_sub) * slice_cols, slice_cols), slice_cols)
@@ -120,6 +122,8 @@
             far_out[...] = term.astype(BF16)
         else:
             leaf[k] = term
+        if k == leaf_order[0]:
+            pl.semaphore_wait(barrier, len(peers))
         if k:
             leaf_send(0, k)
     for j in range(1, CHUNKS):
@@ -169,14 +173,6 @@
     loads[3].wait()
     split_level(2)
     sweep_send(levels - 1)
-    for position, level in ((4, 0), (5, 1)):
-        loads[position].wait()
-        split_level(level)
-        turn_level(level)
-    turn_level(levels - 1)
-    loads[6].wait()
-    inverse_high[...], inverse_low[...] = halves(inverse[...].T)
-    interp_t[...] = interp_value.T
     live = lax.broadcasted_iota(jnp.int32, (chunk, width), 1) < count_ref[0]
 
     up_copies = {}
@@ -212,6 +208,11 @@
         else:
             down_send(up[levels, rows], level, j)
 
+    def prepare(position, level):
+        loads[position].wait()
+        split_level(level)
+        turn_level(level)
+
     def up_own(level):
         up[level + 1] = own_turned(up[level], level)
 
@@ -244,11 +245,17 @@
 
     for j in range(CHUNKS):
         up_start(j)
+    prepare(4, 0)
     up_own(0)
+    prepare(5, 1)
     sweep_take(2)
     step_copies = gather(2, step_map, step_sem)
     every(up_step, 0)
     up_own(1)
+    turn_level(2)
+    loads[6].wait()
+    inverse_high[...], inverse_low[...] = halves(inverse[...].T)
+    interp_t[...] = interp_value.T
     every(up_step, 1)
 
     for copy in step_copies:

time: 56.9 us -> 57.1 us (level)
  no operation moved by 1% of the time
where the time goes in v14:
time: 57.1 us; the launch traced here: 56.9 us
  Pallas kernels  55.5 us (97%)
  local copies, waits for them, and re-layouts  0.8 us (1%)
  between operations  0.66 us (1%)
    pallas_call x1, Pallas kernels, local(): pl.pallas_call(functools.partial(kernel, n_plane, n_z, n_sub, levels), ou...  55.5 us

profile of v14, /device:TPU:1, one launch (start us, length us, event | category | flops | bytes accessed | tf_op | source)
XLA Modules:
  0.0 56.9 jit_solution(15199208298994917457)
XLA Ops:
  0.7 55.5 %shard_map.64 = f32[256,512]{1,0:T(8,128)S(1)} custom-call(bf16[256,512]{1,0:T(8,128)(2,1)} %rhs_hbm.1, bf16[256,256]{1,0:T(8,128)(2,1)} %interp_hbm.1, s32[1]{0:T(128)S(6)} %copy.9.count_ref, f32[3,256,512]{2,1,0:T(8,128)} %butterfly_hbm.1, f32[256,256]{1,0:T(8,128)} %project_hbm.1, f32[256,256]{1,0:T(8,128)} %inverse_hbm.1), custom_call_target="tpu_custom_call" | custom-call | tf_op jit(solution)/shard_map/pallas_call | solution.py:357
  56.1 0.8 %copy.8 = f32[256,512]{1,0:T(8,128)} copy(f32[256,512]{1,0:T(8,128)S(1)} %shard_map.64) | data formatting | bytes 1048576

commit v15 on v13

--- a/solution.py
+++ b/solution.py
@@ -263,13 +263,13 @@
         send(root_part.at[piece_of(k)], root_plane.at[k], plane_sem, k, at_place(k)) for k in range(1, n_plane)]
     up_own(2)
     sweep_take(1)
-    every(up_step, 2)
     total = root_part[piece_of(0)]
     for k, copy in enumerate(plane_copies, 1):
         copy.wait_recv()
         total = total + root_plane[k]
     root_mine[...] = total
     z_copies = [send(root_mine, root_z.at[k], z_sem, k, at_z(k)) for k in range(1, n_z)]
+    every(up_step, 2)
     down[2] = own(up[levels], 2)
     sweep_take(0)
     map_copies = gather(0, root_map, map_sem)

time: 56.9 us -> 57.9 us (1.018)
  Pallas kernels: 55.1 us -> 56.3 us
    pallas_call x1, Pallas kernels: 55.1 us -> 56.3 us  [local(): pl.pallas_call(functools.partial(kernel, n_plane, n_z, n_sub, levels), ou...]
where the time goes in v15:
time: 57.9 us; the launch traced here: 57.8 us
  Pallas kernels  56.3 us (97%)
  local copies, waits for them, and re-layouts  0.8 us (1%)
  between operations  0.66 us (1%)
    pallas_call x1, Pallas kernels, local(): pl.pallas_call(functools.partial(kernel, n_plane, n_z, n_sub, levels), ou...  56.3 us

profile of v15, /device:TPU:1, one launch (start us, length us, event | category | flops | bytes accessed | tf_op | source)
XLA Modules:
  0.0 57.8 jit_solution(5176061973975309594)
XLA Ops:
  0.7 56.3 %shard_map.64 = f32[256,512]{1,0:T(8,128)S(1)} custom-call(bf16[256,512]{1,0:T(8,128)(2,1)} %rhs_hbm.1, bf16[256,256]{1,0:T(8,128)(2,1)} %interp_hbm.1, s32[1]{0:T(128)S(6)} %copy.9.count_ref, f32[3,256,512]{2,1,0:T(8,128)} %butterfly_hbm.1, f32[256,256]{1,0:T(8,128)} %project_hbm.1, f32[256,256]{1,0:T(8,128)} %inverse_hbm.1), custom_call_target="tpu_custom_call" | custom-call | tf_op jit(solution)/shard_map/pallas_call | solution.py:350
  57.0 0.8 %copy.8 = f32[256,512]{1,0:T(8,128)} copy(f32[256,512]{1,0:T(8,128)S(1)} %shard_map.64) | data formatting | bytes 1048576

commit v16 on v13

--- a/solution.py
+++ b/solution.py
@@ -10,7 +10,7 @@
 F32 = jnp.float32
 BF16 = jnp.bfloat16
 MESH = pl.DeviceIdType.MESH
-CHUNKS = 2
+CHUNKS = 4
 NN = (((1,), (0,)), ((), ()))
 NT = (((1,), (1,)), ((), ()))
 

time: 56.9 us -> 57.4 us (level)
  Pallas kernels: 55.1 us -> 55.8 us
    pallas_call x1, Pallas kernels: 55.1 us -> 55.8 us  [local(): pl.pallas_call(functools.partial(kernel, n_plane, n_z, n_sub, levels), ou...]
where the time goes in v16:
time: 57.4 us; the launch traced here: 57.3 us
  Pallas kernels  55.8 us (97%)
  local copies, waits for them, and re-layouts  0.8 us (1%)
  between operations  0.66 us (1%)
    pallas_call x1, Pallas kernels, local(): pl.pallas_call(functools.partial(kernel, n_plane, n_z, n_sub, levels), ou...  55.8 us

profile of v16, /device:TPU:1, one launch (start us, length us, event | category | flops | bytes accessed | tf_op | source)
XLA Modules:
  0.0 57.3 jit_solution(93273483374374401)
XLA Ops:
  0.7 55.8 %shard_map.64 = f32[256,512]{1,0:T(8,128)S(1)} custom-call(bf16[256,512]{1,0:T(8,128)(2,1)} %rhs_hbm.1, bf16[256,256]{1,0:T(8,128)(2,1)} %interp_hbm.1, s32[1]{0:T(128)S(6)} %copy.9.count_ref, f32[3,256,512]{2,1,0:T(8,128)} %butterfly_hbm.1, f32[256,256]{1,0:T(8,128)} %project_hbm.1, f32[256,256]{1,0:T(8,128)} %inverse_hbm.1), custom_call_target="tpu_custom_call" | custom-call | tf_op jit(solution)/shard_map/pallas_call | solution.py:350
  56.5 0.8 %copy.8 = f32[256,512]{1,0:T(8,128)} copy(f32[256,512]{1,0:T(8,128)S(1)} %shard_map.64) | data formatting | bytes 1048576
